TPU v7x, 32 devices: a whole 2x2x4 slice. The times are simulated.
32 devices in a mesh: blk: 16 (over z, y, x), chan: 2 (over core).
Axes of the slice: x: 2, y: 2, z: 4, core: 2. Of those that a mesh axis runs over, the one named last changes fastest.
Arguments:
- inputs: bfloat16 [128, 64, 512], P('chan', 'blk'), may hold values from -6 to 6
- w_first: bfloat16 [3, 3, 128, 128], P(None, None, 'chan'), may hold values from -0.1875 to 0.1875
- w_second: bfloat16 [3, 3, 128, 128], P(None, None, 'chan'), may hold values from -0.1875 to 0.1875
- w_third: bfloat16 [3, 3, 256, 128], P(None, None, 'chan'), may hold values from -0.1875 to 0.1875
- cotangent: bfloat16 [256, 32, 256], P('chan', 'blk'), may hold values from -6 to 6
- mirror: int32 [16], P('blk'), may hold values from 0 to 1
Outputs:
- grad_inputs: bfloat16 [128, 64, 512], P('chan', 'blk')
- grad_first: float32 [3, 3, 128, 128], P(None, None, 'chan')
- grad_second: float32 [3, 3, 128, 128], P(None, None, 'chan')
- grad_third: float32 [3, 3, 256, 128], P(None, None, 'chan')
Inputs may be any that keep to these rules, and one draw needn't show every extreme that they name: `mirror`: 1 marks a tile whose columns are stored in reverse order, 0 a tile stored in the cycle's order.
All inputs are finite; a program needn't handle non-finite values.
Results may differ from a plain program's by a relative error of at most 0.024.
Values may be sent and summed in bfloat16 or wider, within the bound.
No kernel may reach another device: no remote copies, remote signals or barrier semaphores. Data moves between devices by JAX's collectives and lax.ppermute only.
A program may use at most 64 MiB of HBM per device.

v0:
```python
import functools
import math

import jax
import jax.numpy as jnp
from jax import lax
from jax.experimental import pallas as pl
from jax.experimental.pallas import tpu as pltpu
from jax.sharding import PartitionSpec as P

BF = jnp.bfloat16
F32 = jnp.float32
ROOT = math.sqrt(2.0 / math.pi)
CUBIC = 0.044715


def dot(a, b):
    return jnp.dot(a, b, preferred_element_type=F32)


def dot_t(a, b):
    return lax.dot_general(a, b, (((1,), (1,)), ((), ())), preferred_element_type=F32)


def moved_right(v):
    lane = lax.broadcasted_iota(jnp.int32, v.shape, 1)
    return jnp.where(lane == 0, 0.0, pltpu.roll(v, 1, 1))


def moved_left(v):
    lane = lax.broadcasted_iota(jnp.int32, v.shape, 1)
    width = v.shape[1]
    return jnp.where(lane == width - 1, 0.0, pltpu.roll(v, width - 1, 1))


def gelu_parts(v):
    square = v * v
    t = jnp.tanh(v * (ROOT + (ROOT * CUBIC) * square))
    half = 0.5 * v
    return half + half * t, 0.5 + 0.5 * t + half * (1.0 - t * t) * (ROOT + (3.0 * ROOT * CUBIC) * square)


def either(me, own, other):
    return jnp.where(me == 0, own, other), jnp.where(me == 0, other, own)


def weights_kernel(core, own, other, own3, other3, wb1, wb2, wt2, wt1, wt3e, wt3o):
    me = core[0]
    c = own.shape[1]
    h = c // 2
    stack = 4 * c
    for out in (wb1, wb2, wt2, wt1, wt3e, wt3o):
        out[...] = jnp.zeros_like(out)
    for a in range(3):
        for b in range(3):
            tap = a * 3 + b
            at = pl.ds(tap * h, h)
            first = jnp.concatenate(either(me, own[at, :], other[at, :]), axis=0)
            at = pl.ds((9 + tap) * h, h)
            second = jnp.concatenate(either(me, own[at, :], other[at, :]), axis=0)
            for par in range(2):
                at = pl.ds(a * stack + (b + par) * c, c)
                wb1[pl.ds(par * c, c), at] = first
                wb2[pl.ds(par * c, c), at] = second
            turned = second.T
            first_turned = first.T
            half_turned = jnp.where(me == 0, first_turned[:h], first_turned[h:])
            for par in range(2):
                at = pl.ds((2 - a) * stack + (2 - b + par) * c, c)
                wt2[pl.ds(par * c, c), at] = turned
                wt1[pl.ds(par * h, h), at] = half_turned
            at = pl.ds(tap * c, c)
            third = jnp.concatenate([w.T for w in either(me, own3[at, :], other3[at, :])], axis=1)
            par = 0 if b == 1 else 1
            side = 1 if b == 0 else 0
            if a == 1:
                wt3e[pl.ds(par * c, c), pl.ds(side * 2 * c, 2 * c)] = third
            else:
                back = 0 if a == 2 else 1
                wt3o[pl.ds(par * c, c), pl.ds((back * 2 + side) * 2 * c, 2 * c)] = third


def put_stack(ref, base, row):
    c = row.shape[0] // 2
    even, odd = row[:c], row[c:]
    ref[pl.ds(base, c), :] = moved_right(odd).astype(BF)
    ref[pl.ds(base + c, 2 * c), :] = row.astype(BF)
    ref[pl.ds(base + 3 * c, c), :] = moved_left(even).astype(BF)


def run(tasks):
    waiting = None
    for task in tasks:
        if len(task) > 2:
            waiting[0](waiting[1])
            waiting = None
        value = task[0]()
        if waiting:
            waiting[0](waiting[1])
        waiting = (task[1], value)
    waiting[0](waiting[1])


def deal(pieces, grads, tile):
    for k, piece in enumerate(pieces):
        at = piece_at(tile, k)
        base = 0
        for grad in grads:
            size = grad.shape[0] // 4
            piece[pl.ds(base, size), :] = grad[pl.ds(pl.multiple_of(at * size, 16), size), :]
            base += size


def forward_kernel(
    core, own, other, own_before, before, own_after, after, wb1, wb2,
    p0, p1, p2, p3, tx, th1, tu, dz1, dz2, th2, dw3,
):
    me = core[0]
    c = wb1.shape[0] // 2
    h = c // 2
    m = tx.shape[1]
    stack = 4 * c
    rows = own.shape[0] // 3 * 2
    halves = ((me, own_before, own, own_after), (1 - me, before, other, after))

    def source(j, part):
        _, left, here, right = part
        if j < 3:
            return left[j]
        return here[j - 3] if j < 3 + rows else right[j - 3 - rows]

    def input_stack(j):
        for part in halves:
            row = source(j, part)
            even, odd = row[:, :m], row[:, m:]
            blocks = (moved_right(odd.astype(F32)).astype(BF), even, odd, moved_left(even.astype(F32)).astype(BF))
            for k, block in enumerate(blocks):
                tx[pl.ds(pl.multiple_of(j * stack + k * c + part[0] * h, h), h), :] = block

    def cotangent_stack(j):
        for part in halves:
            at, left, here, right = part
            if j == 0:
                row = left[3]
            else:
                row = here[rows + j - 1] if j < 1 + rows // 2 else right[3]
            for k in range(2):
                block = row[:, k * m : (k + 1) * m]
                base = j * stack + at * c + k * h
                tu[pl.ds(pl.multiple_of(base, h), h), :] = block
                tu[pl.ds(pl.multiple_of(base + 2 * c, h), h), :] = moved_left(block.astype(F32)).astype(BF)

    def first_dot(k):
        return dot(wb1[...], tx[pl.ds(k * stack, 3 * stack), :])

    def first_use(k, z):
        act, slope = gelu_parts(z)
        put_stack(th1, k * stack, act)
        if 2 <= k < rows + 2:
            dz1[pl.ds((k - 2) * 2 * c, 2 * c), :] = slope
        if k + 4 < rows + 6:
            input_stack(k + 4)

    def second_dot(k):
        return dot(wb2[...], th1[pl.ds(k * stack, 3 * stack), :])

    def second_use(k, z):
        act, slope = gelu_parts(z)
        dz2[pl.ds(k * 2 * c, 2 * c), :] = slope
        if k <= rows:
            th2[pl.ds(k * 3 * c, c), :] = moved_right(act[c:]).astype(BF)
            th2[pl.ds(k * 3 * c + c, 2 * c), :] = act.astype(BF)

    def third_grad(a):
        total = jnp.zeros((c, 3 * c), F32)
        for r in range(rows // 2):
            mine = tu[pl.ds(pl.multiple_of((r + 1) * stack + me * c, c), c), :]
            total = total + dot_t(mine, th2[pl.ds((2 * r + a) * 3 * c, 3 * c), :])
        return total

    def third_grad_use(a, total):
        for b in range(3):
            dw3[pl.ds((a * 3 + b) * c, c), :] = total[:, b * c : (b + 1) * c].astype(BF)

    z1 = [(functools.partial(first_dot, k), functools.partial(first_use, k)) for k in range(rows + 4)]
    z2 = [(functools.partial(second_dot, k), functools.partial(second_use, k)) for k in range(rows + 2)]
    w3 = [(functools.partial(third_grad, a), functools.partial(third_grad_use, a)) for a in range(3)]
    tasks = z1[:4]
    for k in range(rows):
        tasks += [z2[k], z1[k + 4]]
    tasks += [z2[rows], w3[0], z2[rows + 1], w3[1], w3[2]]
    for j in range(4):
        input_stack(j)
    for j in range(rows // 2 + 2):
        cotangent_stack(j)
    run(tasks)
    deal((p0, p1, p2, p3), (dw3,), core[1])


def backward_kernel(
    core, tx, th1, tu, dz1, dz2, wt2, wt3e, wt3o,
    p0, p1, p2, p3, td1, td2, s2, s1, dw1, dw2,
):
    me = core[0]
    c = wt2.shape[0] // 2
    h = c // 2
    m = tx.shape[1]
    stack = 4 * c
    rows = td1.shape[0] // stack - 4

    def own_channels(ref, index, out, r):
        for par in range(2):
            at = pl.multiple_of(index * stack + (1 + par) * c + me * h, h)
            out[par, pl.ds((rows + 1 - r) * h, h), :] = ref[pl.ds(at, h), :]

    def third_dot(k):
        q = k // 2
        if k % 2 == 0:
            return dot(wt3o[...], tu[pl.ds(q * stack, 2 * stack), :])
        return dot(wt3e[...], tu[pl.ds((q + 1) * stack, stack), :])

    def third_use(k, back):
        put_stack(td2, k * stack, back * dz2[pl.ds(k * 2 * c, 2 * c), :])
        if 1 <= k <= rows:
            own_channels(td2, k, s2, k - 1)

    def back_dot(k):
        return dot(wt2[...], td2[pl.ds(k * stack, 3 * stack), :])

    def back_use(k, back):
        put_stack(td1, (k + 2) * stack, back * dz1[pl.ds(k * 2 * c, 2 * c), :])
        own_channels(td1, k + 2, s1, k)

    def kernel_grad(deltas, stacks, first):
        total = jnp.zeros((3 * h, 3 * c), F32)
        for q in range(rows + 2):
            for par in range(2):
                mine = deltas[par, pl.ds((rows + 1 - q) * h, 3 * h), :]
                total = total + dot_t(mine, stacks[pl.ds((q + first) * stack + par * c, 3 * c), :])
        return total

    def kernel_grad_use(out, total):
        for a in range(3):
            for b in range(3):
                out[pl.ds((a * 3 + b) * h, h), :] = total[a * h : (a + 1) * h, b * c : (b + 1) * c].astype(BF)

    g2 = [(functools.partial(third_dot, k), functools.partial(third_use, k)) for k in range(rows + 2)]
    g1 = [(functools.partial(back_dot, k), functools.partial(back_use, k)) for k in range(rows)]
    w2 = (lambda: kernel_grad(s2, th1, 1), functools.partial(kernel_grad_use, dw2))
    w1 = (lambda: kernel_grad(s1, tx, 2), functools.partial(kernel_grad_use, dw1), "after")
    tasks = g2[:3]
    for k in range(3, rows + 2):
        tasks += [g2[k], g1[k - 3]]
    tasks += [w2, g1[rows - 1], w1]
    for out in (s2, s1):
        for par in range(2):
            out[par, pl.ds(0, 2 * h), :] = jnp.zeros((2 * h, m), BF)
            out[par, pl.ds((rows + 2) * h, 2 * h), :] = jnp.zeros((2 * h, m), BF)
    for k in (0, 1, rows + 2, rows + 3):
        td1[pl.ds(k * stack, stack), :] = jnp.zeros((stack, m), BF)
    run(tasks)
    deal((p0, p1, p2, p3), (dw2, dw1), core[1])


def inputs_kernel(td1, wt1, main, rims):
    h = wt1.shape[0] // 2
    stack = 8 * h
    rows = main.shape[0]
    for k in range(rows + 2):
        back = dot(wt1[...], td1[pl.ds(k * stack, 3 * stack), :])
        flat = jnp.concatenate([back[:h], back[h:]], axis=1)
        if k == 0:
            rims[0] = flat.astype(BF)
        elif k == rows + 1:
            rims[1] = flat.astype(BF)
        else:
            main[k - 1] = flat


def piece_at(tile, k):
    return lax.bitwise_xor(lax.rem(tile, 4), k)


def sum_kernel(*refs):
    total = refs[0][...].astype(F32)
    for piece in refs[1:-1]:
        total = total + piece[...].astype(F32)
    refs[-1][...] = total.astype(BF)


def last_kernel(scale, core, p0, p1, p2, p3, *outs):
    for k, piece in enumerate((p0, p1, p2, p3)):
        at = piece_at(core[1], k)
        base = 0
        for out in outs:
            size = out.shape[0] // 4
            out[pl.ds(pl.multiple_of(at * size, 16), size), :] = piece[pl.ds(base, size), :].astype(F32) * scale
            base += size


def call(body, name, outs, scratch, limit, *args):
    vmem = pl.BlockSpec(memory_space=pltpu.VMEM)
    scalar = pl.BlockSpec(memory_space=pltpu.SMEM)
    return pl.pallas_call(
        body,
        out_shape=tuple(jax.ShapeDtypeStruct(shape, kind) for shape, kind in outs),
        in_specs=[scalar if a.dtype == jnp.int32 else vmem for a in args],
        out_specs=tuple(vmem for _ in outs),
        scratch_shapes=[pltpu.VMEM(shape, kind) for shape, kind in scratch],
        compiler_params=pltpu.CompilerParams(vmem_limit_bytes=limit * 1024 * 1024),
        cost_estimate=pl.CostEstimate(flops=10**6, bytes_accessed=10**5, transcendentals=0),
        name=name,
    )(*args)


def shards(inputs, w_first, w_second, w_third, cotangent, mirror):
    h, rows, cols = inputs.shape
    m = cols // 2
    c = 2 * h
    stack = 4 * c
    tiles = lax.axis_size("blk")
    up = [(i, (i + 1) % tiles) for i in range(tiles)]
    down = [(j, i) for i, j in up]
    core = jnp.stack([lax.axis_index("chan"), lax.axis_index("blk")]).astype(jnp.int32)

    def across(piece):
        return lax.ppermute(piece, "chan", [(0, 1), (1, 0)])

    def swapped(piece, k):
        return lax.ppermute(piece, "blk", [(i, i ^ k) for i in range(tiles)])

    def total(*parts):
        return call(sum_kernel, "sum", [(parts[0].shape, BF)], [], 8, *parts)[0]

    to = lax.broadcasted_iota(jnp.int32, (cols, cols), 1)
    place = 2 * (to % m) + to // m
    place = jnp.where(mirror[0] == 1, cols - 1 - place, place)
    split = (lax.broadcasted_iota(jnp.int32, (cols, cols), 0) == place).astype(BF)
    to = lax.broadcasted_iota(jnp.int32, (m, m), 1)
    place = jnp.where(mirror[0] == 1, m - 1 - to, to)
    turn = (lax.broadcasted_iota(jnp.int32, (m, m), 0) == place).astype(BF)

    x = jnp.einsum("irc,cn->rin", inputs, split, preferred_element_type=F32).astype(BF)
    u = jnp.einsum("orc,cn->ron", cotangent, turn, preferred_element_type=F32).astype(BF)
    u = jnp.concatenate([u[:, :h], u[:, h:]], axis=2)
    before = lax.ppermute(jnp.concatenate([x[rows - 3 :], u[rows // 2 - 1 :]]), "blk", up)
    after = lax.ppermute(jnp.concatenate([x[:3], u[:1]]), "blk", down)
    own = jnp.concatenate([x, u])
    w12 = jnp.concatenate([w.reshape(-1, c) for w in (w_first, w_second)])
    w3 = w_third.reshape(-1, c)
    wb1, wb2, wt2, wt1, wt3e, wt3o = call(
        weights_kernel, "weights",
        [((2 * c, 3 * stack), BF)] * 3 + [((c, 3 * stack), BF), ((2 * c, stack), BF), ((2 * c, 2 * stack), BF)],
        [], 16, core, w12, across(w12), w3, across(w3),
    )

    piece = ((9 * c // 4, c), BF)
    *p_parts, tx, th1, tu, dz1, dz2 = call(
        forward_kernel, "forward",
        [piece] * 4
        + [
            (((rows + 6) * stack, m), BF),
            (((rows + 4) * stack, m), BF),
            (((rows // 2 + 2) * stack, m), BF),
            ((rows * 2 * c, m), F32),
            (((rows + 2) * 2 * c, m), F32),
        ],
        [(((rows + 1) * 3 * c, m), BF), ((9 * c, c), BF)],
        32, core, own, across(own), before, across(before), after, across(after), wb1, wb2,
    )
    p_parts = p_parts[:1] + [swapped(part, k) for k, part in enumerate(p_parts[1:], 1)]
    *q_parts, td1 = call(
        backward_kernel, "backward",
        [piece] * 4 + [(((rows + 4) * stack, m), BF)],
        [
            (((rows + 2) * stack, m), BF),
            ((2, (rows + 4) * h, m), BF),
            ((2, (rows + 4) * h, m), BF),
            ((9 * h, c), BF),
            ((9 * h, c), BF),
        ],
        24, core, tx, th1, tu, dz1, dz2, wt2, wt3e, wt3o,
    )
    q_parts = q_parts[:1] + [swapped(part, k) for k, part in enumerate(q_parts[1:], 1)]
    p_sum = total(*p_parts)
    q_parts, _ = lax.optimization_barrier((q_parts, p_sum))
    q_sum = total(*q_parts)
    bit = 4
    while bit < tiles:
        if bit * 2 >= tiles:
            td1, _ = lax.optimization_barrier((td1, q_sum))
        p_got, q_got = swapped(p_sum, bit), swapped(q_sum, bit)
        p_sum = total(p_sum, p_got)
        ahead = p_sum
        if bit * 2 >= tiles:
            p_all = [p_sum] + [swapped(p_sum, k) for k in range(1, 4)]
            ahead = p_all[1]
        q_got, _ = lax.optimization_barrier((q_got, ahead))
        q_sum = total(q_sum, q_got)
        bit *= 2
    main, rims = call(
        inputs_kernel, "inputs",
        [((rows, h, cols), F32), ((2, h, cols), BF)], [], 16, td1, wt1,
    )
    from_next = lax.ppermute(rims[0], "blk", down)
    from_prev = lax.ppermute(rims[1], "blk", up)
    from_next, from_prev, _ = lax.optimization_barrier((from_next, from_prev, q_sum))
    from_next, from_prev = from_next.astype(F32), from_prev.astype(F32)
    main = jnp.concatenate([main[:1] + from_prev, main[1:-1], main[-1:] + from_next]).astype(BF)
    grad_inputs = jnp.einsum("rin,cn->irc", main, split, preferred_element_type=F32).astype(BF)

    cells = rows * cols * tiles
    (third,) = call(
        functools.partial(last_kernel, 1.0 / math.sqrt(cells // 4)), "third",
        [((9 * c, c), F32)], [], 8, core, *p_all,
    )
    second, first = call(
        functools.partial(last_kernel, 1.0 / math.sqrt(cells)), "last",
        [((9 * h, c), F32), ((9 * h, c), F32)], [], 8, core, q_sum, *[swapped(q_sum, k) for k in range(1, 4)],
    )
    return grad_inputs, first.reshape(3, 3, h, c), second.reshape(3, 3, h, c), third.reshape(3, 3, c, c)


def solution(mesh):
    placed = (
        P("chan", "blk", None),
        P(None, None, "chan", None),
        P(None, None, "chan", None),
        P(None, None, "chan", None),
        P("chan", "blk", None),
        P("blk"),
    )
    return jax.shard_map(
        shards,
        mesh=mesh,
        in_specs=placed,
        out_specs=(
            P("chan", "blk", None),
            P(None, None, "chan", None),
            P(None, None, "chan", None),
            P(None, None, "chan", None),
        ),
        check_vma=False,
    )
```

profile of v0, /device:TPU:0, one launch (start us, length us, event | category | flops | bytes accessed | tf_op | source)
XLA Modules:
  0.0 67.8 jit_solution(13755108216835941262)
XLA Ops:
  0.6 0.0 copy-start
  1.4 1.1 %fusion.2 = bf16[2,128,256]{2,1,0:T(8,128)(2,1)S(1)} fusion(bf16[128,2,256]{2,1,0:T(2,128)(2,1)} %param.10, s32[256]{0:T(256)S(1)} %iota_select_fusion), kind=kOutput, calls=%fused_computation.6 | convolution fusion | flops 33685504 | bytes 263168 | tf_op jit(solution)/shard_map/orc,cn->ron/dot_general | solution.py:344
  2.5 0.4 fusion
  2.9 0.0 copy-start.2
  2.9 0.0 copy-start.3
  2.9 0.0 copy-start.1
  3.0 3.0 %collective-permute-start.1 = (bf16[4,64,512]{2,1,0:T(8,128)(2,1)S(1)}, bf16[4,64,512]{2,1,0:T(8,128)(2,1)S(1)}, u32[]{:S(2)}, u32[]{:S(2)}) collective-permute-start(bf16[4,64,512]{2,1,0:T(8,128)(2,1)S(1)} %pad_maximum_fusion.2), channel_id=1, source_target_pairs={{0,2},{2,4},{4,6},{6,8},{8,10},{10,12},{12,14},{14,16},{16,18},{18... | collective-permute-start | bytes 786440 | tf_op jit(solution)/shard_map/ppermute | solution.py:346
  6.0 4.1 %collective-permute-start.3 = (bf16[4,64,512]{2,1,0:T(8,128)(2,1)S(1)}, bf16[4,64,512]{2,1,0:T(8,128)(2,1)S(1)}, u32[]{:S(2)}, u32[]{:S(2)}) collective-permute-start(bf16[4,64,512]{2,1,0:T(8,128)(2,1)S(1)} %fusion.5), channel_id=1, source_target_pairs={{2,0},{4,2},{6,4},{8,6},{10,8},{12,10},{14,12},{16,14},{18,16},{20... | collective-permute-start | bytes 786440 | tf_op jit(solution)/shard_map/ppermute | solution.py:347
  10.1 0.1 collective-permute-start
  10.3 0.5 collective-permute-start.5
  10.8 0.1 collective-permute-start.6
  10.9 6.3 %collective-permute-done.1.own_before = bf16[4,64,512]{2,1,0:T(8,128)(2,1)S(1)} collective-permute-done((bf16[4,64,512]{2,1,0:T(8,128)(2,1)S(1)}, bf16[4,64,512]{2,1,0:T(8,128)(2,1)S(1)}, u32[]{:S(2)}, u32[]{:S(2)}) %collective-permute-start.1) | collective-permute-done | bytes 262176 | tf_op jit(solution)/shard_map/ppermute | solution.py:346
  17.2 1.9 %collective-permute-done.3.own_after = bf16[4,64,512]{2,1,0:T(8,128)(2,1)S(1)} collective-permute-done((bf16[4,64,512]{2,1,0:T(8,128)(2,1)S(1)}, bf16[4,64,512]{2,1,0:T(8,128)(2,1)S(1)}, u32[]{:S(2)}, u32[]{:S(2)}) %collective-permute-start.3) | collective-permute-done | bytes 262176 | tf_op jit(solution)/shard_map/ppermute | solution.py:347
  19.1 0.0 collective-permute-start.4
  19.2 0.1 pad_add_fusion.core
  19.2 0.0 collective-permute-done.5.other
  19.2 1.2 %weights.1 = (bf16[256,1536]{1,0:T(8,128)(2,1)S(1)}, bf16[256,1536]{1,0:T(8,128)(2,1)S(1)}, bf16[256,1536]{1,0:T(8,128)(2,1)S(1)}, bf16[128,1536]{1,0:T(8,128)(2...) custom-call(s32[2]{0:T(128)S(1)} %pad_add_fusion.core, bf16[1152,128]{1,0:T(8,128)(2,1)S(1)} %pad_maximum_fusion.own, ...), custom_call_target="tpu_custom_call" | custom-call | flops 1000000 | bytes 100000 | tf_op jit(solution)/shard_map/weights/pallas_call | solution.py:304
  20.4 0.0 collective-permute-done.2.before
  20.4 0.3 collective-permute-done.4.after
  20.7 5.4 %forward.1 = (bf16[288,128]{1,0:T(8,128)(2,1)S(1)}, bf16[288,128]{1,0:T(8,128)(2,1)S(1)}, bf16[288,128]{1,0:T(8,128)(2,1)S(1)}, bf16[288,128]{1,0:T(8,128)(2,1)S...) custom-call(s32[2]{0:T(128)S(1)} %pad_add_fusion.core, ...), custom_call_target="tpu_custom_call" | custom-call | flops 1000000 | bytes 100000 | tf_op jit(solution)/shard_map/forward/pallas_call | solution.py:304
  26.1 1.6 %collective-permute-start.10 = (bf16[288,128]{1,0:T(8,128)(2,1)S(1)}, bf16[288,128]{1,0:T(8,128)(2,1)S(1)}, u32[]{:S(2)}, u32[]{:S(2)}) collective-permute-start(bf16[288,128]{1,0:T(8,128)(2,1)S(1)} %get-tuple-element.53), channel_id=1, source_target_pairs={{0,2},{2,0},{4,6},{6,4},{8,10},{10,8},{12,14},{14,12},{16,18},{18,... | collective-permute-start | bytes 221192 | tf_op jit(solution)/shard_map/ppermute | solution.py:330
  27.6 0.4 collective-permute-start.11
  28.1 1.5 %collective-permute-start.12 = (bf16[288,128]{1,0:T(8,128)(2,1)S(1)}, bf16[288,128]{1,0:T(8,128)(2,1)S(1)}, u32[]{:S(2)}, u32[]{:S(2)}) collective-permute-start(bf16[288,128]{1,0:T(8,128)(2,1)S(1)} %get-tuple-element.55), channel_id=1, source_target_pairs={{0,6},{2,4},{4,2},{6,0},{8,14},{10,12},{12,10},{14,8},{16,22},{18,... | collective-permute-start | bytes 221192 | tf_op jit(solution)/shard_map/ppermute | solution.py:330
  29.6 4.3 %backward.1 = (bf16[288,128]{1,0:T(8,128)(2,1)S(1)}, bf16[288,128]{1,0:T(8,128)(2,1)S(1)}, bf16[288,128]{1,0:T(8,128)(2,1)S(1)}, bf16[288,128]{1,0:T(8,128)(2,1)S(1)}, bf16[4096,256]{1,0:T(8,128)(2,1)S(1)}) custom-call(s32[2]{0:T(128)S(1)} %pad_add_fusion.core, bf16[5120,256]{1,0:T(8,128)(2,1)S(1)} %get-tuple-element.39.tx, ...), custom_call_target="tpu_custom_call" | custom-call | flops 1000000 | bytes 100000 | tf_op jit(solution)/shard_map/backward/pallas_call | solution.py:304
  33.9 1.6 %collective-permute-start.7 = (bf16[288,128]{1,0:T(8,128)(2,1)S(1)}, bf16[288,128]{1,0:T(8,128)(2,1)S(1)}, u32[]{:S(2)}, u32[]{:S(2)}) collective-permute-start(bf16[288,128]{1,0:T(8,128)(2,1)S(1)} %get-tuple-element.49), channel_id=1, source_target_pairs={{0,2},{2,0},{4,6},{6,4},{8,10},{10,8},{12,14},{14,12},{16,18},{18,... | collective-permute-start | bytes 221192 | tf_op jit(solution)/shard_map/ppermute | solution.py:330
  35.5 0.5 collective-permute-start.8
  35.9 1.5 %collective-permute-start.9 = (bf16[288,128]{1,0:T(8,128)(2,1)S(1)}, bf16[288,128]{1,0:T(8,128)(2,1)S(1)}, u32[]{:S(2)}, u32[]{:S(2)}) collective-permute-start(bf16[288,128]{1,0:T(8,128)(2,1)S(1)} %get-tuple-element.51), channel_id=1, source_target_pairs={{0,6},{2,4},{4,2},{6,0},{8,14},{10,12},{12,10},{14,8},{16,22},{18,... | collective-permute-start | bytes 221192 | tf_op jit(solution)/shard_map/ppermute | solution.py:330
  37.5 1.6 %collective-permute-start.14 = (bf16[288,128]{1,0:T(8,128)(2,1)S(1)}, bf16[288,128]{1,0:T(8,128)(2,1)S(1)}, u32[]{:S(2)}, u32[]{:S(2)}) collective-permute-start(bf16[288,128]{1,0:T(8,128)(2,1)S(1)} %sum.6.refs_0_), channel_id=1, source_target_pairs={{0,8},{2,10},{4,12},{6,14},{8,0},{10,2},{12,4},{14,6},{16,24},{18,... | collective-permute-start | bytes 221192 | tf_op jit(solution)/shard_map/ppermute | solution.py:330
  39.2 1.1 %collective-permute-done.8.refs_2_ = bf16[288,128]{1,0:T(8,128)(2,1)S(1)} collective-permute-done((bf16[288,128]{1,0:T(8,128)(2,1)S(1)}, bf16[288,128]{1,0:T(8,128)(2,1)S(1)}, u32[]{:S(2)}, u32[]{:S(2)}) %collective-permute-start.8) | collective-permute-done | bytes 73760 | tf_op jit(solution)/shard_map/ppermute | solution.py:330
  40.3 0.9 %collective-permute-done.9.refs_3_ = bf16[288,128]{1,0:T(8,128)(2,1)S(1)} collective-permute-done((bf16[288,128]{1,0:T(8,128)(2,1)S(1)}, bf16[288,128]{1,0:T(8,128)(2,1)S(1)}, u32[]{:S(2)}, u32[]{:S(2)}) %collective-permute-start.9) | collective-permute-done | bytes 73760 | tf_op jit(solution)/shard_map/ppermute | solution.py:330
  41.2 1.3 %collective-permute-start.13 = (bf16[288,128]{1,0:T(8,128)(2,1)S(1)}, bf16[288,128]{1,0:T(8,128)(2,1)S(1)}, u32[]{:S(2)}, u32[]{:S(2)}) collective-permute-start(bf16[288,128]{1,0:T(8,128)(2,1)S(1)} %sum.7.refs_0_), channel_id=1, source_target_pairs={{0,8},{2,10},{4,12},{6,14},{8,0},{10,2},{12,4},{14,6},{16,24},{18,... | collective-permute-start | bytes 221192 | tf_op jit(solution)/shard_map/ppermute | solution.py:330
  42.5 2.6 %collective-permute-start.18 = (bf16[288,128]{1,0:T(8,128)(2,1)S(1)}, bf16[288,128]{1,0:T(8,128)(2,1)S(1)}, u32[]{:S(2)}, u32[]{:S(2)}) collective-permute-start(bf16[288,128]{1,0:T(8,128)(2,1)S(1)} %sum.8.refs_0_), channel_id=1, source_target_pairs={{0,16},{2,18},{4,20},{6,22},{8,24},{10,26},{12,28},{14,30},{16,0},... | collective-permute-start | bytes 221192 | tf_op jit(solution)/shard_map/ppermute | solution.py:330
  45.2 0.5 collective-permute-done.13.refs_1_
  45.7 2.4 %collective-permute-start.17 = (bf16[288,128]{1,0:T(8,128)(2,1)S(1)}, bf16[288,128]{1,0:T(8,128)(2,1)S(1)}, u32[]{:S(2)}, u32[]{:S(2)}) collective-permute-start(bf16[288,128]{1,0:T(8,128)(2,1)S(1)} %sum.9.refs_0_), channel_id=1, source_target_pairs={{0,16},{2,18},{4,20},{6,22},{8,24},{10,26},{12,28},{14,30},{16,0},... | collective-permute-start | bytes 221192 | tf_op jit(solution)/shard_map/ppermute | solution.py:330
  48.1 0.8 %inputs.1 = (f32[4,64,512]{2,1,0:T(8,128)S(1)}, bf16[2,64,512]{2,1,0:T(8,128)(2,1)S(1)}) custom-call(bf16[4096,256]{1,0:T(8,128)(2,1)S(1)} %get-tuple-element.61.td1, bf16[128,1536]{1,0:T(8,128)(2,1)S(1)} %get-tuple-element.62.wt1), custom_call_target="tpu_custom_call" | custom-call | flops 1000000 | bytes 100000 | tf_op jit(solution)/shard_map/inputs/pallas_call | solution.py:304
  48.9 0.9 %collective-permute-done.18.refs_1_ = bf16[288,128]{1,0:T(8,128)(2,1)S(1)} collective-permute-done((bf16[288,128]{1,0:T(8,128)(2,1)S(1)}, bf16[288,128]{1,0:T(8,128)(2,1)S(1)}, u32[]{:S(2)}, u32[]{:S(2)}) %collective-permute-start.18) | collective-permute-done | bytes 73760 | tf_op jit(solution)/shard_map/ppermute | solution.py:330
  49.8 1.4 %collective-permute-start.19 = (bf16[288,128]{1,0:T(8,128)(2,1)S(1)}, bf16[288,128]{1,0:T(8,128)(2,1)S(1)}, u32[]{:S(2)}, u32[]{:S(2)}) collective-permute-start(bf16[288,128]{1,0:T(8,128)(2,1)S(1)} %sum.10.p0), channel_id=1, source_target_pairs={{0,2},{2,0},{4,6},{6,4},{8,10},{10,8},{12,14},{14,12},{16,18},{18,... | collective-permute-start | bytes 221192 | tf_op jit(solution)/shard_map/ppermute | solution.py:330
  51.2 0.8 %collective-permute-start.16 = (bf16[64,512]{1,0:T(8,128)(2,1)S(1)}, bf16[64,512]{1,0:T(8,128)(2,1)S(1)}, u32[]{:S(2)}, u32[]{:S(2)}) collective-permute-start(bf16[64,512]{1,0:T(8,128)(2,1)S(1)} %get-tuple-element.78), channel_id=1, source_target_pairs={{0,2},{2,4},{4,6},{6,8},{8,10},{10,12},{12,14},{14,16},{16,18},{18... | collective-permute-start | bytes 196616 | tf_op jit(solution)/shard_map/ppermute | solution.py:406
  52.0 4.9 %collective-permute-start.15 = (bf16[64,512]{1,0:T(8,128)(2,1)S(1)}, bf16[64,512]{1,0:T(8,128)(2,1)S(1)}, u32[]{:S(2)}, u32[]{:S(2)}) collective-permute-start(bf16[64,512]{1,0:T(8,128)(2,1)S(1)} %get-tuple-element.79), channel_id=1, source_target_pairs={{2,0},{4,2},{6,4},{8,6},{10,8},{12,10},{14,12},{16,14},{18,16},{20... | collective-permute-start | bytes 196616 | tf_op jit(solution)/shard_map/ppermute | solution.py:405
  56.9 0.1 collective-permute-start.24
  57.0 0.1 collective-permute-start.23
  57.2 2.9 %collective-permute-start.22 = (bf16[288,128]{1,0:T(8,128)(2,1)S(1)}, bf16[288,128]{1,0:T(8,128)(2,1)S(1)}, u32[]{:S(2)}, u32[]{:S(2)}) collective-permute-start(bf16[288,128]{1,0:T(8,128)(2,1)S(1)} %sum.11.p0), channel_id=1, source_target_pairs={{0,6},{2,4},{4,2},{6,0},{8,14},{10,12},{12,10},{14,8},{16,22},{18,... | collective-permute-start | bytes 221192 | tf_op jit(solution)/shard_map/ppermute | solution.py:330
  60.0 2.0 %collective-permute-start.21 = (bf16[288,128]{1,0:T(8,128)(2,1)S(1)}, bf16[288,128]{1,0:T(8,128)(2,1)S(1)}, u32[]{:S(2)}, u32[]{:S(2)}) collective-permute-start(bf16[288,128]{1,0:T(8,128)(2,1)S(1)} %sum.11.p0), channel_id=1, source_target_pairs={{0,4},{2,6},{4,0},{6,2},{8,12},{10,14},{12,8},{14,10},{16,20},{18,... | collective-permute-start | bytes 221192 | tf_op jit(solution)/shard_map/ppermute | solution.py:330
  62.1 0.4 fusion.1
  62.5 0.9 %copy.12 = bf16[64,4,512]{2,1,0:T(4,128)(2,1)} copy(bf16[64,4,512]{2,0,1:T(8,128)(2,1)S(1)} %fusion.1) | data formatting | bytes 524288
  63.4 1.4 %third.1 = f32[1152,128]{1,0:T(8,128)} custom-call(s32[2]{0:T(128)S(1)} %pad_add_fusion.core, bf16[288,128]{1,0:T(8,128)(2,1)S(1)} %sum.10.p0, bf16[288,128]{1,0:T(8,128)(2,1)S(1)} %collective-permute-done.19.p1, bf16[288,128]{1,0:T(8,128)(2,1)S(1)} %collective-permute-done.23.p2, bf16[288,128]{1,0:T(8,128)(2,1)S(1)} %collective-permute-done.24.p3), custom_call_target="tpu_custom_call" | custom-call | flops 1000000 | bytes 100000 | tf_op jit(solution)/shard_map/third/pallas_call | solution.py:304
  64.8 1.6 %collective-permute-done.20.p1 = bf16[288,128]{1,0:T(8,128)(2,1)S(1)} collective-permute-done((bf16[288,128]{1,0:T(8,128)(2,1)S(1)}, bf16[288,128]{1,0:T(8,128)(2,1)S(1)}, u32[]{:S(2)}, u32[]{:S(2)}) %collective-permute-start.20) | collective-permute-done | bytes 73760 | tf_op jit(solution)/shard_map/ppermute | solution.py:330
  66.4 1.4 %last.1 = (f32[576,128]{1,0:T(8,128)}, f32[576,128]{1,0:T(8,128)}) custom-call(s32[2]{0:T(128)S(1)} %pad_add_fusion.core, bf16[288,128]{1,0:T(8,128)(2,1)S(1)} %sum.11.p0, bf16[288,128]{1,0:T(8,128)(2,1)S(1)} %collective-permute-done.20.p1, bf16[288,128]{1,0:T(8,128)(2,1)S(1)} %collective-permute-done.21.p2, bf16[288,128]{1,0:T(8,128)(2,1)S(1)} %collective-permute-done.22.p3), custom_call_target="tpu_custom_call" | custom-call | flops 1000000 | bytes 100000 | tf_op jit(solution)/shard_map/last/pallas_call | solution.py:304
  (41 shorter events, 0.4 us)
Async XLA Ops:
  0.6 1.9 %copy-start = (bf16[64,4,512]{2,1,0:T(4,128)(2,1)S(1)}, bf16[64,4,512]{2,1,0:T(4,128)(2,1)}, u32[]{:S(2)}) copy-start(bf16[64,4,512]{2,1,0:T(4,128)(2,1)} %param.6) | copy-start | bytes 786436
  2.9 7.3 %copy-start.2 = (bf16[3,3,64,128]{3,2,1,0:T(8,128)(2,1)S(1)}, bf16[3,3,64,128]{3,2,1,0:T(8,128)(2,1)}, u32[]{:S(2)}) copy-start(bf16[3,3,64,128]{3,2,1,0:T(8,128)(2,1)} %param.8) | copy-start | bytes 442372
  2.9 7.3 %copy-start.3 = (bf16[3,3,64,128]{3,2,1,0:T(8,128)(2,1)S(1)}, bf16[3,3,64,128]{3,2,1,0:T(8,128)(2,1)}, u32[]{:S(2)}) copy-start(bf16[3,3,64,128]{3,2,1,0:T(8,128)(2,1)} %param.7) | copy-start | bytes 442372
  2.9 7.9 %copy-start.1 = (bf16[3,3,128,128]{3,2,1,0:T(8,128)(2,1)S(1)}, bf16[3,3,128,128]{3,2,1,0:T(8,128)(2,1)}, u32[]{:S(2)}) copy-start(bf16[3,3,128,128]{3,2,1,0:T(8,128)(2,1)} %param.9) | copy-start | bytes 884740
  3.0 14.2 %collective-permute-start.1 = (bf16[4,64,512]{2,1,0:T(8,128)(2,1)S(1)}, bf16[4,64,512]{2,1,0:T(8,128)(2,1)S(1)}, u32[]{:S(2)}, u32[]{:S(2)}) collective-permute-start(bf16[4,64,512]{2,1,0:T(8,128)(2,1)S(1)} %pad_maximum_fusion.2), channel_id=1, source_target_pairs={{0,2},{2,4},{4,6},{6,8},{8,10},{10,12},{12,14},{14,16},{16,18},{18... | collective-permute-start | bytes 786440 | tf_op jit(solution)/shard_map/ppermute | solution.py:346
  6.0 13.1 %collective-permute-start.3 = (bf16[4,64,512]{2,1,0:T(8,128)(2,1)S(1)}, bf16[4,64,512]{2,1,0:T(8,128)(2,1)S(1)}, u32[]{:S(2)}, u32[]{:S(2)}) collective-permute-start(bf16[4,64,512]{2,1,0:T(8,128)(2,1)S(1)} %fusion.5), channel_id=1, source_target_pairs={{2,0},{4,2},{6,4},{8,6},{10,8},{12,10},{14,12},{16,14},{18,16},{20... | collective-permute-start | bytes 786440 | tf_op jit(solution)/shard_map/ppermute | solution.py:347
  10.1 10.3 %collective-permute-start = (bf16[6,64,512]{2,1,0:T(8,128)(2,1)S(1)}, bf16[6,64,512]{2,1,0:T(8,128)(2,1)S(1)}, u32[]{:S(2)}, u32[]{:S(2)}) collective-permute-start(bf16[6,64,512]{2,1,0:T(8,128)(2,1)S(1)} %maximum_maximum_fusion.own), channel_id=1, source_target_pairs={{0,1},{1,0},{2,3},{3,2},{4,5},{5,4},{6,7},{7,6},{8,9},{9,8},{10,11... | collective-permute-start | bytes 1179656 | tf_op jit(solution)/shard_map/ppermute | solution.py:327
  10.3 9.0 %collective-permute-start.5 = (bf16[1152,128]{1,0:T(8,128)(2,1)S(1)}, bf16[1152,128]{1,0:T(8,128)(2,1)S(1)}, u32[]{:S(2)}, u32[]{:S(2)}) collective-permute-start(bf16[1152,128]{1,0:T(8,128)(2,1)S(1)} %pad_maximum_fusion.own), channel_id=1, source_target_pairs={{0,1},{1,0},{2,3},{3,2},{4,5},{5,4},{6,7},{7,6},{8,9},{9,8},{10,11... | collective-permute-start | bytes 884744 | tf_op jit(solution)/shard_map/ppermute | solution.py:327
  10.8 8.4 %collective-permute-start.6 = (bf16[1152,128]{1,0:T(8,128)(2,1)S(1)}, bf16[1152,128]{1,0:T(8,128)(2,1)S(1)}, u32[]{:S(2)}, u32[]{:S(2)}) collective-permute-start(bf16[1152,128]{1,0:T(8,128)(2,1)S(1)} %bitcast.32), channel_id=1, source_target_pairs={{0,1},{1,0},{2,3},{3,2},{4,5},{5,4},{6,7},{7,6},{8,9},{9,8},{10,11... | collective-permute-start | bytes 884744 | tf_op jit(solution)/shard_map/ppermute | solution.py:327
  17.2 3.2 %collective-permute-start.2 = (bf16[4,64,512]{2,1,0:T(8,128)(2,1)S(1)}, bf16[4,64,512]{2,1,0:T(8,128)(2,1)S(1)}, u32[]{:S(2)}, u32[]{:S(2)}) collective-permute-start(bf16[4,64,512]{2,1,0:T(8,128)(2,1)S(1)} %collective-permute-done.1.own_before), channel_id=1, source_target_pairs={{0,1},{1,0},{2,3},{3,2},{4,5},{5,4},{6,7},{7,6},{8,9},{9,8},{10,11... | collective-permute-start | bytes 786440 | tf_op jit(solution)/shard_map/ppermute | solution.py:327
  19.1 1.5 %collective-permute-start.4 = (bf16[4,64,512]{2,1,0:T(8,128)(2,1)S(1)}, bf16[4,64,512]{2,1,0:T(8,128)(2,1)S(1)}, u32[]{:S(2)}, u32[]{:S(2)}) collective-permute-start(bf16[4,64,512]{2,1,0:T(8,128)(2,1)S(1)} %collective-permute-done.3.own_after), channel_id=1, source_target_pairs={{0,1},{1,0},{2,3},{3,2},{4,5},{5,4},{6,7},{7,6},{8,9},{9,8},{10,11... | collective-permute-start | bytes 786440 | tf_op jit(solution)/shard_map/ppermute | solution.py:327
  26.1 9.9 %collective-permute-start.10 = (bf16[288,128]{1,0:T(8,128)(2,1)S(1)}, bf16[288,128]{1,0:T(8,128)(2,1)S(1)}, u32[]{:S(2)}, u32[]{:S(2)}) collective-permute-start(bf16[288,128]{1,0:T(8,128)(2,1)S(1)} %get-tuple-element.53), channel_id=1, source_target_pairs={{0,2},{2,0},{4,6},{6,4},{8,10},{10,8},{12,14},{14,12},{16,18},{18,... | collective-permute-start | bytes 221192 | tf_op jit(solution)/shard_map/ppermute | solution.py:330
  27.6 9.8 %collective-permute-start.11 = (bf16[288,128]{1,0:T(8,128)(2,1)S(1)}, bf16[288,128]{1,0:T(8,128)(2,1)S(1)}, u32[]{:S(2)}, u32[]{:S(2)}) collective-permute-start(bf16[288,128]{1,0:T(8,128)(2,1)S(1)} %get-tuple-element.54), channel_id=1, source_target_pairs={{0,4},{2,6},{4,0},{6,2},{8,12},{10,14},{12,8},{14,10},{16,20},{18,... | collective-permute-start | bytes 221192 | tf_op jit(solution)/shard_map/ppermute | solution.py:330
  28.1 9.4 %collective-permute-start.12 = (bf16[288,128]{1,0:T(8,128)(2,1)S(1)}, bf16[288,128]{1,0:T(8,128)(2,1)S(1)}, u32[]{:S(2)}, u32[]{:S(2)}) collective-permute-start(bf16[288,128]{1,0:T(8,128)(2,1)S(1)} %get-tuple-element.55), channel_id=1, source_target_pairs={{0,6},{2,4},{4,2},{6,0},{8,14},{10,12},{12,10},{14,8},{16,22},{18,... | collective-permute-start | bytes 221192 | tf_op jit(solution)/shard_map/ppermute | solution.py:330
  33.9 5.3 %collective-permute-start.7 = (bf16[288,128]{1,0:T(8,128)(2,1)S(1)}, bf16[288,128]{1,0:T(8,128)(2,1)S(1)}, u32[]{:S(2)}, u32[]{:S(2)}) collective-permute-start(bf16[288,128]{1,0:T(8,128)(2,1)S(1)} %get-tuple-element.49), channel_id=1, source_target_pairs={{0,2},{2,0},{4,6},{6,4},{8,10},{10,8},{12,14},{14,12},{16,18},{18,... | collective-permute-start | bytes 221192 | tf_op jit(solution)/shard_map/ppermute | solution.py:330
  35.5 4.8 %collective-permute-start.8 = (bf16[288,128]{1,0:T(8,128)(2,1)S(1)}, bf16[288,128]{1,0:T(8,128)(2,1)S(1)}, u32[]{:S(2)}, u32[]{:S(2)}) collective-permute-start(bf16[288,128]{1,0:T(8,128)(2,1)S(1)} %get-tuple-element.50), channel_id=1, source_target_pairs={{0,4},{2,6},{4,0},{6,2},{8,12},{10,14},{12,8},{14,10},{16,20},{18,... | collective-permute-start | bytes 221192 | tf_op jit(solution)/shard_map/ppermute | solution.py:330
  35.9 5.3 %collective-permute-start.9 = (bf16[288,128]{1,0:T(8,128)(2,1)S(1)}, bf16[288,128]{1,0:T(8,128)(2,1)S(1)}, u32[]{:S(2)}, u32[]{:S(2)}) collective-permute-start(bf16[288,128]{1,0:T(8,128)(2,1)S(1)} %get-tuple-element.51), channel_id=1, source_target_pairs={{0,6},{2,4},{4,2},{6,0},{8,14},{10,12},{12,10},{14,8},{16,22},{18,... | collective-permute-start | bytes 221192 | tf_op jit(solution)/shard_map/ppermute | solution.py:330
  37.5 5.0 %collective-permute-start.14 = (bf16[288,128]{1,0:T(8,128)(2,1)S(1)}, bf16[288,128]{1,0:T(8,128)(2,1)S(1)}, u32[]{:S(2)}, u32[]{:S(2)}) collective-permute-start(bf16[288,128]{1,0:T(8,128)(2,1)S(1)} %sum.6.refs_0_), channel_id=1, source_target_pairs={{0,8},{2,10},{4,12},{6,14},{8,0},{10,2},{12,4},{14,6},{16,24},{18,... | collective-permute-start | bytes 221192 | tf_op jit(solution)/shard_map/ppermute | solution.py:330
  41.2 4.5 %collective-permute-start.13 = (bf16[288,128]{1,0:T(8,128)(2,1)S(1)}, bf16[288,128]{1,0:T(8,128)(2,1)S(1)}, u32[]{:S(2)}, u32[]{:S(2)}) collective-permute-start(bf16[288,128]{1,0:T(8,128)(2,1)S(1)} %sum.7.refs_0_), channel_id=1, source_target_pairs={{0,8},{2,10},{4,12},{6,14},{8,0},{10,2},{12,4},{14,6},{16,24},{18,... | collective-permute-start | bytes 221192 | tf_op jit(solution)/shard_map/ppermute | solution.py:330
  42.5 7.3 %collective-permute-start.18 = (bf16[288,128]{1,0:T(8,128)(2,1)S(1)}, bf16[288,128]{1,0:T(8,128)(2,1)S(1)}, u32[]{:S(2)}, u32[]{:S(2)}) collective-permute-start(bf16[288,128]{1,0:T(8,128)(2,1)S(1)} %sum.8.refs_0_), channel_id=1, source_target_pairs={{0,16},{2,18},{4,20},{6,22},{8,24},{10,26},{12,28},{14,30},{16,0},... | collective-permute-start | bytes 221192 | tf_op jit(solution)/shard_map/ppermute | solution.py:330
  45.7 11.3 %collective-permute-start.17 = (bf16[288,128]{1,0:T(8,128)(2,1)S(1)}, bf16[288,128]{1,0:T(8,128)(2,1)S(1)}, u32[]{:S(2)}, u32[]{:S(2)}) collective-permute-start(bf16[288,128]{1,0:T(8,128)(2,1)S(1)} %sum.9.refs_0_), channel_id=1, source_target_pairs={{0,16},{2,18},{4,20},{6,22},{8,24},{10,26},{12,28},{14,30},{16,0},... | collective-permute-start | bytes 221192 | tf_op jit(solution)/shard_map/ppermute | solution.py:330
  49.8 7.3 %collective-permute-start.19 = (bf16[288,128]{1,0:T(8,128)(2,1)S(1)}, bf16[288,128]{1,0:T(8,128)(2,1)S(1)}, u32[]{:S(2)}, u32[]{:S(2)}) collective-permute-start(bf16[288,128]{1,0:T(8,128)(2,1)S(1)} %sum.10.p0), channel_id=1, source_target_pairs={{0,2},{2,0},{4,6},{6,4},{8,10},{10,8},{12,14},{14,12},{16,18},{18,... | collective-permute-start | bytes 221192 | tf_op jit(solution)/shard_map/ppermute | solution.py:330
  51.2 8.8 %collective-permute-start.16 = (bf16[64,512]{1,0:T(8,128)(2,1)S(1)}, bf16[64,512]{1,0:T(8,128)(2,1)S(1)}, u32[]{:S(2)}, u32[]{:S(2)}) collective-permute-start(bf16[64,512]{1,0:T(8,128)(2,1)S(1)} %get-tuple-element.78), channel_id=1, source_target_pairs={{0,2},{2,4},{4,6},{6,8},{8,10},{10,12},{12,14},{14,16},{16,18},{18... | collective-permute-start | bytes 196616 | tf_op jit(solution)/shard_map/ppermute | solution.py:406
  52.0 10.1 %collective-permute-start.15 = (bf16[64,512]{1,0:T(8,128)(2,1)S(1)}, bf16[64,512]{1,0:T(8,128)(2,1)S(1)}, u32[]{:S(2)}, u32[]{:S(2)}) collective-permute-start(bf16[64,512]{1,0:T(8,128)(2,1)S(1)} %get-tuple-element.79), channel_id=1, source_target_pairs={{2,0},{4,2},{6,4},{8,6},{10,8},{12,10},{14,12},{16,14},{18,16},{20... | collective-permute-start | bytes 196616 | tf_op jit(solution)/shard_map/ppermute | solution.py:405
  56.9 6.5 %collective-permute-start.24 = (bf16[288,128]{1,0:T(8,128)(2,1)S(1)}, bf16[288,128]{1,0:T(8,128)(2,1)S(1)}, u32[]{:S(2)}, u32[]{:S(2)}) collective-permute-start(bf16[288,128]{1,0:T(8,128)(2,1)S(1)} %sum.10.p0), channel_id=1, source_target_pairs={{0,6},{2,4},{4,2},{6,0},{8,14},{10,12},{12,10},{14,8},{16,22},{18,... | collective-permute-start | bytes 221192 | tf_op jit(solution)/shard_map/ppermute | solution.py:330
  57.0 6.4 %collective-permute-start.23 = (bf16[288,128]{1,0:T(8,128)(2,1)S(1)}, bf16[288,128]{1,0:T(8,128)(2,1)S(1)}, u32[]{:S(2)}, u32[]{:S(2)}) collective-permute-start(bf16[288,128]{1,0:T(8,128)(2,1)S(1)} %sum.10.p0), channel_id=1, source_target_pairs={{0,4},{2,6},{4,0},{6,2},{8,12},{10,14},{12,8},{14,10},{16,20},{18,... | collective-permute-start | bytes 221192 | tf_op jit(solution)/shard_map/ppermute | solution.py:330
  57.2 7.7 %collective-permute-start.22 = (bf16[288,128]{1,0:T(8,128)(2,1)S(1)}, bf16[288,128]{1,0:T(8,128)(2,1)S(1)}, u32[]{:S(2)}, u32[]{:S(2)}) collective-permute-start(bf16[288,128]{1,0:T(8,128)(2,1)S(1)} %sum.11.p0), channel_id=1, source_target_pairs={{0,6},{2,4},{4,2},{6,0},{8,14},{10,12},{12,10},{14,8},{16,22},{18,... | collective-permute-start | bytes 221192 | tf_op jit(solution)/shard_map/ppermute | solution.py:330
  60.0 4.8 %collective-permute-start.21 = (bf16[288,128]{1,0:T(8,128)(2,1)S(1)}, bf16[288,128]{1,0:T(8,128)(2,1)S(1)}, u32[]{:S(2)}, u32[]{:S(2)}) collective-permute-start(bf16[288,128]{1,0:T(8,128)(2,1)S(1)} %sum.11.p0), channel_id=1, source_target_pairs={{0,4},{2,6},{4,0},{6,2},{8,12},{10,14},{12,8},{14,10},{16,20},{18,... | collective-permute-start | bytes 221192 | tf_op jit(solution)/shard_map/ppermute | solution.py:330
  62.1 4.4 %collective-permute-start.20 = (bf16[288,128]{1,0:T(8,128)(2,1)S(1)}, bf16[288,128]{1,0:T(8,128)(2,1)S(1)}, u32[]{:S(2)}, u32[]{:S(2)}) collective-permute-start(bf16[288,128]{1,0:T(8,128)(2,1)S(1)} %sum.11.p0), channel_id=1, source_target_pairs={{0,2},{2,0},{4,6},{6,4},{8,10},{10,8},{12,14},{14,12},{16,18},{18,... | collective-permute-start | bytes 221192 | tf_op jit(solution)/shard_map/ppermute | solution.py:330
where the time goes:
time: 68 us; the launch traced here: 67.8 us
  starting transfers between devices  35 us (51%)
  Pallas kernels  14.6 us (21%)
  waiting for transfers between devices  13.6 us (20%)
  matrix products  1.89 us (3%)
  between operations  1.62 us (2%)
  local copies, waits for them, and re-layouts  1 us (1%)
    ppermute x16, starting transfers between devices, swapped(): return lax.ppermute(piece, 'blk', [(i, i ^ k) for i in range(tiles)])  21.5 us
    pallas_call x12, Pallas kernels, call(): pl.pallas_call(body, out_shape=tuple((jax.ShapeDtypeStruct(shape, kind) f...  14.6 us
    ppermute x1, waiting for transfers between devices, shards(): lax.ppermute(jnp.concatenate([x[rows - 3:], u[rows // 2 - 1:]]), 'blk', up)  6.3 us
    ppermute x16, waiting for transfers between devices, swapped(): return lax.ppermute(piece, 'blk', [(i, i ^ k) for i in range(tiles)])  5.04 us
    ppermute x1, starting transfers between devices, shards(): from_next = lax.ppermute(rims[0], 'blk', down)  4.92 us
    ppermute x1, starting transfers between devices, shards(): after = lax.ppermute(jnp.concatenate([x[:3], u[:1]]), 'blk', down)  4.06 us
    ppermute x1, starting transfers between devices, shards(): lax.ppermute(jnp.concatenate([x[rows - 3:], u[rows // 2 - 1:]]), 'blk', up)  2.99 us
    ppermute x1, waiting for transfers between devices, shards(): after = lax.ppermute(jnp.concatenate([x[:3], u[:1]]), 'blk', down)  1.94 us
  transfers between devices with their start and end apart: 25, of which 8 were waited for; matrix products, arithmetic and copies ran while one was open for 2% of the time, Pallas kernels for 11%

commit v1 on v0

v1 whole, which is shorter than its diff:
```python
import functools
import math

import jax
import jax.numpy as jnp
from jax import lax
from jax.experimental import pallas as pl
from jax.experimental.pallas import tpu as pltpu
from jax.sharding import PartitionSpec as P

BF = jnp.bfloat16
F32 = jnp.float32
ROOT = math.sqrt(2.0 / math.pi)
CUBIC = 0.044715


def dot(a, b):
    return jnp.dot(a, b, preferred_element_type=F32)


def dot_t(a, b):
    return lax.dot_general(a, b, (((1,), (1,)), ((), ())), preferred_element_type=F32)


def moved_right(v):
    lane = lax.broadcasted_iota(jnp.int32, v.shape, 1)
    return jnp.where(lane == 0, 0.0, pltpu.roll(v, 1, 1))


def moved_left(v):
    lane = lax.broadcasted_iota(jnp.int32, v.shape, 1)
    width = v.shape[1]
    return jnp.where(lane == width - 1, 0.0, pltpu.roll(v, width - 1, 1))


def gelu_parts(v):
    square = v * v
    t = jnp.tanh(v * (ROOT + (ROOT * CUBIC) * square))
    half = 0.5 * v
    return half + half * t, 0.5 + 0.5 * t + half * (1.0 - t * t) * (ROOT + (3.0 * ROOT * CUBIC) * square)


def either(me, own, other):
    return jnp.where(me == 0, own, other), jnp.where(me == 0, other, own)


def put_weights(me, own1, other1, own2, other2, own3, other3, wb1, wb2, wt2, wt1, wt3e, wt3o):
    c = own1.shape[1]
    h = c // 2
    stack = 4 * c
    for out in (wb1, wb2, wt2, wt1, wt3e, wt3o):
        out[...] = jnp.zeros_like(out)
    for a in range(3):
        for b in range(3):
            tap = a * 3 + b
            at = pl.ds(tap * h, h)
            first = jnp.concatenate(either(me, own1[at, :], other1[at, :]), axis=0)
            second = jnp.concatenate(either(me, own2[at, :], other2[at, :]), axis=0)
            for par in range(2):
                at = pl.ds(a * stack + (b + par) * c, c)
                wb1[pl.ds(par * c, c), at] = first
                wb2[pl.ds(par * c, c), at] = second
            turned = second.T
            first_turned = first.T
            half_turned = jnp.where(me == 0, first_turned[:h], first_turned[h:])
            for par in range(2):
                at = pl.ds((2 - a) * stack + (2 - b + par) * c, c)
                wt2[pl.ds(par * c, c), at] = turned
                wt1[pl.ds(par * h, h), at] = half_turned
            at = pl.ds(tap * c, c)
            third = jnp.concatenate([w.T for w in either(me, own3[at, :], other3[at, :])], axis=1)
            par = 0 if b == 1 else 1
            side = 1 if b == 0 else 0
            if a == 1:
                wt3e[pl.ds(par * c, c), pl.ds(side * 2 * c, 2 * c)] = third
            else:
                back = 0 if a == 2 else 1
                wt3o[pl.ds(par * c, c), pl.ds((back * 2 + side) * 2 * c, 2 * c)] = third


def put_stack(ref, base, row):
    c = row.shape[0] // 2
    even, odd = row[:c], row[c:]
    ref[pl.ds(base, c), :] = moved_right(odd).astype(BF)
    ref[pl.ds(base + c, 2 * c), :] = row.astype(BF)
    ref[pl.ds(base + 3 * c, c), :] = moved_left(even).astype(BF)


def run(tasks):
    waiting = None
    for task in tasks:
        value = task[0]()
        if waiting:
            waiting[0](waiting[1])
        waiting = (task[1], value)
    waiting[0](waiting[1])


def deal(pieces, grads, tile):
    for k, piece in enumerate(pieces):
        at = piece_at(tile, k)
        base = 0
        for grad in grads:
            size = grad.shape[0] // 4
            piece[pl.ds(base, size), :] = grad[pl.ds(pl.multiple_of(at * size, 16), size), :]
            base += size


def put_input(ref, base, me, own, other):
    m = own.shape[1] // 2
    h = own.shape[0]
    for at, row in ((me, own), (1 - me, other)):
        even, odd = row[:, :m], row[:, m:]
        blocks = (moved_right(odd.astype(F32)).astype(BF), even, odd, moved_left(even.astype(F32)).astype(BF))
        for k, block in enumerate(blocks):
            ref[pl.ds(pl.multiple_of(base + k * 2 * h + at * h, h), h), :] = block


def put_cotangent(ref, base, me, own, other):
    m = own.shape[1] // 2
    h = own.shape[0]
    for at, row in ((me, own), (1 - me, other)):
        for k in range(2):
            block = row[:, k * m : (k + 1) * m]
            to = base + at * 2 * h + k * h
            ref[pl.ds(pl.multiple_of(to, h), h), :] = block
            ref[pl.ds(pl.multiple_of(to + 4 * h, h), h), :] = moved_left(block.astype(F32)).astype(BF)


def inner_kernel(
    core, own, other, w1, other1, w2, other2, w3, other3,
    wb1, wb2, wt2, wt1, wt3e, wt3o, tx, tu, th1, dz1, g2,
):
    me = core[0]
    c = wb1.shape[0] // 2
    stack = 4 * c
    rows = own.shape[0] // 3 * 2
    put_weights(me, w1, other1, w2, other2, w3, other3, wb1, wb2, wt2, wt1, wt3e, wt3o)
    for r in range(rows):
        put_input(tx, r * stack, me, own[r], other[r])
    for r in range(rows // 2):
        put_cotangent(tu, r * stack, me, own[rows + r], other[rows + r])

    def first_dot(r):
        return dot(wb1[...], tx[pl.ds((r - 1) * stack, 3 * stack), :])

    def first_use(r, z):
        act, slope = gelu_parts(z)
        put_stack(th1, (r - 1) * stack, act)
        dz1[pl.ds((r - 1) * 2 * c, 2 * c), :] = slope

    def third_dot(r):
        if r % 2 == 0:
            return dot(wt3e[...], tu[pl.ds(r // 2 * stack, stack), :])
        return dot(wt3o[...], tu[pl.ds(r // 2 * stack, 2 * stack), :])

    def third_use(r, back):
        g2[pl.ds(r * 2 * c, 2 * c), :] = back

    z1 = [(functools.partial(first_dot, r), functools.partial(first_use, r)) for r in range(1, rows - 1)]
    back = [(functools.partial(third_dot, r), functools.partial(third_use, r)) for r in range(rows - 1)]
    run(z1 + back)


def main_kernel(
    core, own_before, before, own_after, after, wb1, wb2, wt2, wt3e, wt3o, txi, tui, th1i, dz1i, g2i,
    p0, p1, p2, p3, td1, txo, tuo, th1o, dz1o, dz2, th2, td2, s2, s1, dw1, dw2, dw3,
):
    me = core[0]
    c = wb1.shape[0] // 2
    h = c // 2
    m = td1.shape[1]
    stack = 4 * c
    rows = td1.shape[0] // stack - 4

    def input_at(r):
        if 0 <= r < rows:
            return txi, r * stack
        return txo, (r + 3 if r < 0 else r - rows + 3) * stack

    def first_at(r):
        if 1 <= r < rows - 1:
            return th1i, (r - 1) * stack
        return th1o, (r + 2 if r < 1 else r - rows + 4) * stack

    def cotangent_at(r):
        if 0 <= r < rows // 2:
            return tui, r * stack
        return tuo, 0 if r < 0 else stack

    def window(at, first, count):
        places = [at(r) for r in range(first, first + count)]
        return jnp.concatenate([ref[pl.ds(base, stack), :] for ref, base in places], axis=0)

    def own_channels(ref, index, out, r):
        for par in range(2):
            at = pl.multiple_of(index * stack + (1 + par) * c + me * h, h)
            out[par, pl.ds((rows + 1 - r) * h, h), :] = ref[pl.ds(at, h), :]

    def first_dot(r):
        return dot(wb1[...], window(input_at, r - 1, 3))

    def first_use(r, z):
        act, slope = gelu_parts(z)
        ref, base = first_at(r)
        put_stack(ref, base, act)
        if r in (0, rows - 1):
            dz1o[pl.ds((r > 0) * 2 * c, 2 * c), :] = slope

    def second_dot(r):
        return dot(wb2[...], window(first_at, r - 1, 3))

    def second_use(r, z):
        act, slope = gelu_parts(z)
        k = r + 1
        dz2[pl.ds(k * 2 * c, 2 * c), :] = slope
        if r < rows:
            th2[pl.ds(k * 3 * c, c), :] = moved_right(act[c:]).astype(BF)
            th2[pl.ds(k * 3 * c + c, 2 * c), :] = act.astype(BF)

    def third_dot(r):
        if 0 <= r < rows - 1:
            return None
        if r % 2 == 0:
            return dot(wt3e[...], window(cotangent_at, r // 2, 1))
        return dot(wt3o[...], window(cotangent_at, (r - 1) // 2 if r > 0 else -1, 2))

    def third_use(r, back):
        if back is None:
            back = g2i[pl.ds(r * 2 * c, 2 * c), :]
        k = r + 1
        put_stack(td2, k * stack, back * dz2[pl.ds(k * 2 * c, 2 * c), :])
        if 0 <= r < rows:
            own_channels(td2, k, s2, r)

    def back_dot(r):
        return dot(wt2[...], td2[pl.ds(r * stack, 3 * stack), :])

    def back_use(r, back):
        if 0 < r < rows - 1:
            slope = dz1i[pl.ds((r - 1) * 2 * c, 2 * c), :]
        else:
            slope = dz1o[pl.ds((r > 0) * 2 * c, 2 * c), :]
        put_stack(td1, (r + 2) * stack, back * slope)
        own_channels(td1, r + 2, s1, r)

    def third_grad(a):
        total = jnp.zeros((c, 3 * c), F32)
        for r in range(rows // 2):
            mine = tui[pl.ds(pl.multiple_of(r * stack + me * c, c), c), :]
            total = total + dot_t(mine, th2[pl.ds((2 * r + a) * 3 * c, 3 * c), :])
        return total

    def third_grad_use(a, total):
        for b in range(3):
            dw3[pl.ds((a * 3 + b) * c, c), :] = total[:, b * c : (b + 1) * c].astype(BF)

    def kernel_grad(deltas, at):
        total = jnp.zeros((3 * h, 3 * c), F32)
        for q in range(rows + 2):
            ref, base = at(q - 1)
            for par in range(2):
                mine = deltas[par, pl.ds((rows + 1 - q) * h, 3 * h), :]
                total = total + dot_t(mine, ref[pl.ds(base + par * c, 3 * c), :])
        return total

    def kernel_grad_use(out, total):
        for a in range(3):
            for b in range(3):
                out[pl.ds((a * 3 + b) * h, h), :] = total[a * h : (a + 1) * h, b * c : (b + 1) * c].astype(BF)

    def task(does, uses, r):
        return functools.partial(does, r), functools.partial(uses, r)

    z1 = {r: task(first_dot, first_use, r) for r in range(-2, rows + 2)}
    z2 = {r: task(second_dot, second_use, r) for r in range(-1, rows + 1)}
    g2 = {r: task(third_dot, third_use, r) for r in range(-1, rows + 1)}
    g1 = {r: task(back_dot, back_use, r) for r in range(rows)}
    w3 = {a: task(third_grad, third_grad_use, a) for a in range(3)}
    w2 = (lambda: kernel_grad(s2, first_at), functools.partial(kernel_grad_use, dw2))
    w1 = (lambda: kernel_grad(s1, input_at), functools.partial(kernel_grad_use, dw1))
    tasks = [z1[-2], z1[-1], z1[0], z1[rows - 1], z2[-1], z1[rows], z2[0], z1[rows + 1]]
    tasks += [z2[r] for r in range(1, rows)] + [g2[-1], z2[rows]] + [g2[r] for r in range(rows)]
    tasks += [w3[0], g1[0], g2[rows], w3[1]] + [g1[r] for r in range(1, rows - 1)] + [w3[2], g1[rows - 1], w2, w1]

    for r in (-3, -2, -1):
        ref, base = input_at(r)
        put_input(ref, base, me, own_before[r + 3], before[r + 3])
    for r in range(rows, rows + 3):
        ref, base = input_at(r)
        put_input(ref, base, me, own_after[r - rows], after[r - rows])
    put_cotangent(tuo, 0, me, own_before[3], before[3])
    put_cotangent(tuo, stack, me, own_after[3], after[3])
    for out in (s2, s1):
        for par in range(2):
            out[par, pl.ds(0, 2 * h), :] = jnp.zeros((2 * h, m), BF)
            out[par, pl.ds((rows + 2) * h, 2 * h), :] = jnp.zeros((2 * h, m), BF)
    for k in (0, 1, rows + 2, rows + 3):
        td1[pl.ds(k * stack, stack), :] = jnp.zeros((stack, m), BF)
    run(tasks)
    deal((p0, p1, p2, p3), (dw3, dw2, dw1), core[1])


def inputs_kernel(td1, wt1, main, rims):
    h = wt1.shape[0] // 2
    stack = 8 * h
    rows = main.shape[0]
    for k in range(rows + 2):
        back = dot(wt1[...], td1[pl.ds(k * stack, 3 * stack), :])
        flat = jnp.concatenate([back[:h], back[h:]], axis=1)
        if k == 0:
            rims[0] = flat.astype(BF)
        elif k == rows + 1:
            rims[1] = flat.astype(BF)
        else:
            main[k - 1] = flat


def piece_at(tile, k):
    return lax.bitwise_xor(lax.rem(tile, 4), k)


def sum_kernel(*refs):
    total = refs[0][...].astype(F32)
    for piece in refs[1:-1]:
        total = total + piece[...].astype(F32)
    refs[-1][...] = total.astype(BF)


def last_kernel(scales, core, p0, p1, p2, p3, *outs):
    for k, piece in enumerate((p0, p1, p2, p3)):
        at = piece_at(core[1], k)
        base = 0
        for out, scale in zip(outs, scales):
            size = out.shape[0] // 4
            out[pl.ds(pl.multiple_of(at * size, 16), size), :] = piece[pl.ds(base, size), :].astype(F32) * scale
            base += size


def call(body, name, outs, scratch, limit, *args):
    vmem = pl.BlockSpec(memory_space=pltpu.VMEM)
    scalar = pl.BlockSpec(memory_space=pltpu.SMEM)
    return pl.pallas_call(
        body,
        out_shape=tuple(jax.ShapeDtypeStruct(shape, kind) for shape, kind in outs),
        in_specs=[scalar if a.dtype == jnp.int32 else vmem for a in args],
        out_specs=tuple(vmem for _ in outs),
        scratch_shapes=[pltpu.VMEM(shape, kind) for shape, kind in scratch],
        compiler_params=pltpu.CompilerParams(vmem_limit_bytes=limit * 1024 * 1024),
        cost_estimate=pl.CostEstimate(flops=10**6, bytes_accessed=10**5, transcendentals=0),
        name=name,
    )(*args)


def shards(inputs, w_first, w_second, w_third, cotangent, mirror):
    h, rows, cols = inputs.shape
    m = cols // 2
    c = 2 * h
    stack = 4 * c
    tiles = lax.axis_size("blk")
    up = [(i, (i + 1) % tiles) for i in range(tiles)]
    down = [(j, i) for i, j in up]
    core = jnp.stack([lax.axis_index("chan"), lax.axis_index("blk")]).astype(jnp.int32)

    def across(piece):
        return lax.ppermute(piece, "chan", [(0, 1), (1, 0)])

    def swapped(piece, k):
        return lax.ppermute(piece, "blk", [(i, i ^ k) for i in range(tiles)])

    def total(*parts):
        return call(sum_kernel, "sum", [(parts[0].shape, BF)], [], 8, *parts)[0]

    to = lax.broadcasted_iota(jnp.int32, (cols, cols), 1)
    place = 2 * (to % m) + to // m
    place = jnp.where(mirror[0] == 1, cols - 1 - place, place)
    split = (lax.broadcasted_iota(jnp.int32, (cols, cols), 0) == place).astype(BF)
    to = lax.broadcasted_iota(jnp.int32, (m, m), 1)
    place = jnp.where(mirror[0] == 1, m - 1 - to, to)
    turn = (lax.broadcasted_iota(jnp.int32, (m, m), 0) == place).astype(BF)

    x = jnp.einsum("irc,cn->rin", inputs, split, preferred_element_type=F32).astype(BF)
    u = jnp.einsum("orc,cn->ron", cotangent, turn, preferred_element_type=F32).astype(BF)
    u = jnp.concatenate([u[:, :h], u[:, h:]], axis=2)
    before = lax.ppermute(jnp.concatenate([x[rows - 3 :], u[rows // 2 - 1 :]]), "blk", up)
    after = lax.ppermute(jnp.concatenate([x[:3], u[:1]]), "blk", down)
    own = jnp.concatenate([x, u])
    weights = []
    for w in (w_first, w_second, w_third):
        w = w.reshape(-1, c)
        weights += [w, across(w)]
    wb1, wb2, wt2, wt1, wt3e, wt3o, tx, tu, th1, dz1, g2 = call(
        inner_kernel, "inner",
        [
            ((2 * c, 3 * stack), BF),
            ((2 * c, 3 * stack), BF),
            ((2 * c, 3 * stack), BF),
            ((c, 3 * stack), BF),
            ((2 * c, stack), BF),
            ((2 * c, 2 * stack), BF),
            ((rows * stack, m), BF),
            ((rows // 2 * stack, m), BF),
            (((rows - 2) * stack, m), BF),
            (((rows - 2) * 2 * c, m), F32),
            (((rows - 1) * 2 * c, m), F32),
        ],
        [], 24, core, own, across(own), *weights,
    )
    before, after, _ = lax.optimization_barrier((before, after, g2))

    size = 9 * (c + 2 * h) // 4
    *parts, td1 = call(
        main_kernel, "main",
        [((size, c), BF)] * 4 + [(((rows + 4) * stack, m), BF)],
        [
            ((6 * stack, m), BF),
            ((2 * stack, m), BF),
            ((6 * stack, m), BF),
            ((2 * 2 * c, m), F32),
            (((rows + 2) * 2 * c, m), F32),
            (((rows + 1) * 3 * c, m), BF),
            (((rows + 2) * stack, m), BF),
            ((2, (rows + 4) * h, m), BF),
            ((2, (rows + 4) * h, m), BF),
            ((9 * h, c), BF),
            ((9 * h, c), BF),
            ((9 * c, c), BF),
        ],
        32, core, before, across(before), after, across(after), wb1, wb2, wt2, wt3e, wt3o, tx, tu, th1, dz1, g2,
    )
    mine = total(parts[0], *[swapped(part, k) for k, part in enumerate(parts[1:], 1)])
    bit = 4
    while bit < tiles:
        if bit * 2 >= tiles:
            mine, td1 = lax.optimization_barrier((mine, td1))
        mine = total(mine, swapped(mine, bit))
        bit *= 2
    main, rims = call(
        inputs_kernel, "inputs",
        [((rows, h, cols), F32), ((2, h, cols), BF)], [], 16, td1, wt1,
    )
    from_next = lax.ppermute(rims[0], "blk", down)
    from_prev = lax.ppermute(rims[1], "blk", up)
    from_next, from_prev, _ = lax.optimization_barrier((from_next, from_prev, mine))
    from_next, from_prev = from_next.astype(F32), from_prev.astype(F32)
    main = jnp.concatenate([main[:1] + from_prev, main[1:-1], main[-1:] + from_next]).astype(BF)
    grad_inputs = jnp.einsum("rin,cn->irc", main, split, preferred_element_type=F32).astype(BF)

    cells = rows * cols * tiles
    wide, narrow = 1.0 / math.sqrt(cells // 4), 1.0 / math.sqrt(cells)
    third, second, first = call(
        functools.partial(last_kernel, (wide, narrow, narrow)), "last",
        [((9 * c, c), F32), ((9 * h, c), F32), ((9 * h, c), F32)], [], 16,
        core, mine, *[swapped(mine, k) for k in range(1, 4)],
    )
    return grad_inputs, first.reshape(3, 3, h, c), second.reshape(3, 3, h, c), third.reshape(3, 3, c, c)


def solution(mesh):
    placed = (
        P("chan", "blk", None),
        P(None, None, "chan", None),
        P(None, None, "chan", None),
        P(None, None, "chan", None),
        P("chan", "blk", None),
        P("blk"),
    )
    return jax.shard_map(
        shards,
        mesh=mesh,
        in_specs=placed,
        out_specs=(
            P("chan", "blk", None),
            P(None, None, "chan", None),
            P(None, None, "chan", None),
            P(None, None, "chan", None),
        ),
        check_vma=False,
    )
```

time: 68 us -> 64.1 us (0.943)
  starting transfers between devices: 35 us -> 25.4 us
  waiting for transfers between devices: 13.6 us -> 21.8 us
  Pallas kernels: 14.6 us -> 12.2 us
    ppermute x16 -> x8, starting transfers between devices: 21.5 us -> 11.2 us  [swapped(): return lax.ppermute(piece, 'blk', [(i, i ^ k) for i in range(tiles)])]
    ppermute x16 -> x8, waiting for transfers between devices: 5.04 us -> 13.3 us  [swapped(): return lax.ppermute(piece, 'blk', [(i, i ^ k) for i in range(tiles)])]
    pallas_call x12 -> x7, Pallas kernels: 14.6 us -> 12.2 us  [call(): pl.pallas_call(body, out_shape=tuple((jax.ShapeDtypeStruct(shape, kind) f...]
    ppermute x5 -> x6, waiting for transfers between devices: 0.27 us -> 2.54 us  [across(): return lax.ppermute(piece, 'chan', [(0, 1), (1, 0)])]
    ppermute x1, waiting for transfers between devices: 6.3 us -> 4.03 us  [shards(): lax.ppermute(jnp.concatenate([x[rows - 3:], u[rows // 2 - 1:]]), 'blk', up)]
    ppermute x5 -> x6, starting transfers between devices: 0.7 us -> 1.77 us  [across(): return lax.ppermute(piece, 'chan', [(0, 1), (1, 0)])]
  transfers between devices with their start and end apart: 25 -> 18, of which waited for: 8 -> 11; matrix products, arithmetic and copies ran while one was open for 2% -> 5% of each run, Pallas kernels for 11% -> 5%
where the time goes in v1:
time: 64.1 us; the launch traced here: 63.9 us
  starting transfers between devices  25.4 us (40%)
  waiting for transfers between devices  21.8 us (34%)
  Pallas kernels  12.2 us (19%)
  matrix products  1.89 us (3%)
  between operations  1.48 us (2%)
  local copies, waits for them, and re-layouts  1 us (2%)
    ppermute x8, waiting for transfers between devices, swapped(): return lax.ppermute(piece, 'blk', [(i, i ^ k) for i in range(tiles)])  13.3 us
    pallas_call x7, Pallas kernels, call(): pl.pallas_call(body, out_shape=tuple((jax.ShapeDtypeStruct(shape, kind) f...  12.2 us
    ppermute x8, starting transfers between devices, swapped(): return lax.ppermute(piece, 'blk', [(i, i ^ k) for i in range(tiles)])  11.2 us
    ppermute x1, starting transfers between devices, shards(): from_next = lax.ppermute(rims[0], 'blk', down)  5.09 us
    ppermute x1, starting transfers between devices, shards(): after = lax.ppermute(jnp.concatenate([x[:3], u[:1]]), 'blk', down)  4.07 us
    ppermute x1, waiting for transfers between devices, shards(): lax.ppermute(jnp.concatenate([x[rows - 3:], u[rows // 2 - 1:]]), 'blk', up)  4.03 us
    ppermute x1, starting transfers between devices, shards(): lax.ppermute(jnp.concatenate([x[rows - 3:], u[rows // 2 - 1:]]), 'blk', up)  2.62 us
    ppermute x6, waiting for transfers between devices, across(): return lax.ppermute(piece, 'chan', [(0, 1), (1, 0)])  2.54 us
  transfers between devices with their start and end apart: 18, of which 11 were waited for; matrix products, arithmetic and copies ran while one was open for 5% of the time, Pallas kernels for 5%

profile of v1, /device:TPU:0, one launch (start us, length us, event | category | flops | bytes accessed | tf_op | source)
XLA Modules:
  0.0 63.9 jit_solution(18357885761527405662)
XLA Ops:
  0.6 0.0 copy-start
  0.6 0.5 collective-permute-start.3
  1.2 0.1 collective-permute-start.5
  1.9 1.1 %fusion.2 = bf16[2,128,256]{2,1,0:T(8,128)(2,1)S(1)} fusion(bf16[128,2,256]{2,1,0:T(2,128)(2,1)} %param.10, s32[256]{0:T(256)S(1)} %iota_select_fusion), kind=kOutput, calls=%fused_computation.6 | convolution fusion | flops 33685504 | bytes 263168 | tf_op jit(solution)/shard_map/orc,cn->ron/dot_general | solution.py:383
  3.1 0.4 fusion
  3.5 0.0 copy-start.3
  3.5 0.0 copy-start.1
  3.5 0.0 copy-start.2
  3.5 0.5 collective-permute-start.2
  4.1 2.6 %collective-permute-start = (bf16[4,64,512]{2,1,0:T(8,128)(2,1)S(1)}, bf16[4,64,512]{2,1,0:T(8,128)(2,1)S(1)}, u32[]{:S(2)}, u32[]{:S(2)}) collective-permute-start(bf16[4,64,512]{2,1,0:T(8,128)(2,1)S(1)} %pad_maximum_fusion.1), channel_id=1, source_target_pairs={{0,2},{2,4},{4,6},{6,8},{8,10},{10,12},{12,14},{14,16},{16,18},{18... | collective-permute-start | bytes 786440 | tf_op jit(solution)/shard_map/ppermute | solution.py:385
  6.7 4.1 %collective-permute-start.1 = (bf16[4,64,512]{2,1,0:T(8,128)(2,1)S(1)}, bf16[4,64,512]{2,1,0:T(8,128)(2,1)S(1)}, u32[]{:S(2)}, u32[]{:S(2)}) collective-permute-start(bf16[4,64,512]{2,1,0:T(8,128)(2,1)S(1)} %fusion.5), channel_id=1, source_target_pairs={{2,0},{4,2},{6,4},{8,6},{10,8},{12,10},{14,12},{16,14},{18,16},{20... | collective-permute-start | bytes 786440 | tf_op jit(solution)/shard_map/ppermute | solution.py:386
  10.8 0.0 collective-permute-done.3.other1
  10.8 0.2 collective-permute-start.4
  11.0 0.1 pad_add_fusion.core
  11.1 1.1 %collective-permute-done.4.other2 = bf16[576,128]{1,0:T(8,128)(2,1)S(1)} collective-permute-done((bf16[576,128]{1,0:T(8,128)(2,1)S(1)}, bf16[576,128]{1,0:T(8,128)(2,1)S(1)}, u32[]{:S(2)}, u32[]{:S(2)}) %collective-permute-start.4) | collective-permute-done | bytes 147488 | tf_op jit(solution)/shard_map/ppermute | solution.py:366
  12.2 0.0 collective-permute-done.5.other3
  12.2 0.0 collective-permute-done.2.other
  12.2 2.3 %inner.1 = (bf16[256,1536]{1,0:T(8,128)(2,1)S(1)}, bf16[256,1536]{1,0:T(8,128)(2,1)S(1)}, bf16[256,1536]{1,0:T(8,128)(2,1)S(1)}, bf16[128,1536]{1,0:T(8,128)(2,1...) custom-call(s32[2]{0:T(128)S(1)} %pad_add_fusion.core, ...), custom_call_target="tpu_custom_call" | custom-call | flops 1000000 | bytes 100000 | tf_op jit(solution)/shard_map/inner/pallas_call | solution.py:343
  14.5 4.0 %collective-permute-done.own_before = bf16[4,64,512]{2,1,0:T(8,128)(2,1)S(1)} collective-permute-done((bf16[4,64,512]{2,1,0:T(8,128)(2,1)S(1)}, bf16[4,64,512]{2,1,0:T(8,128)(2,1)S(1)}, u32[]{:S(2)}, u32[]{:S(2)}) %collective-permute-start) | collective-permute-done | bytes 262176 | tf_op jit(solution)/shard_map/ppermute | solution.py:385
  18.5 1.9 %collective-permute-done.1.own_after = bf16[4,64,512]{2,1,0:T(8,128)(2,1)S(1)} collective-permute-done((bf16[4,64,512]{2,1,0:T(8,128)(2,1)S(1)}, bf16[4,64,512]{2,1,0:T(8,128)(2,1)S(1)}, u32[]{:S(2)}, u32[]{:S(2)}) %collective-permute-start.1) | collective-permute-done | bytes 262176 | tf_op jit(solution)/shard_map/ppermute | solution.py:386
  20.5 0.0 collective-permute-start.6
  20.5 0.5 collective-permute-start.7
  21.0 1.0 %collective-permute-done.6.before = bf16[4,64,512]{2,1,0:T(8,128)(2,1)S(1)} collective-permute-done((bf16[4,64,512]{2,1,0:T(8,128)(2,1)S(1)}, bf16[4,64,512]{2,1,0:T(8,128)(2,1)S(1)}, u32[]{:S(2)}, u32[]{:S(2)}) %collective-permute-start.6) | collective-permute-done | bytes 262176 | tf_op jit(solution)/shard_map/ppermute | solution.py:366
  22.0 0.4 collective-permute-done.7.after
  22.4 7.3 %main.1 = (bf16[576,128]{1,0:T(8,128)(2,1)S(1)}, bf16[576,128]{1,0:T(8,128)(2,1)S(1)}, bf16[576,128]{1,0:T(8,128)(2,1)S(1)}, bf16[576,128]{1,0:T(8,128)(2,1)S(1)}, bf16[4096,256]{1,0:T(8,128)(2,1)S(1)}) custom-call(s32[2]{0:T(128)S(1)} %pad_add_fusion.core, bf16[4,64,512]{2,1,0:T(8,128)(2,1)S(1)} %collective-permute-done.own_before, ...), custom_call_target="tpu_custom_call" | custom-call | flops 1000000 | bytes 100000 | tf_op jit(solution)/shard_map/main/pallas_call | solution.py:343
  29.7 1.6 %collective-permute-start.8 = (bf16[576,128]{1,0:T(8,128)(2,1)S(1)}, bf16[576,128]{1,0:T(8,128)(2,1)S(1)}, u32[]{:S(2)}, u32[]{:S(2)}) collective-permute-start(bf16[576,128]{1,0:T(8,128)(2,1)S(1)} %get-tuple-element.44), channel_id=1, source_target_pairs={{0,2},{2,0},{4,6},{6,4},{8,10},{10,8},{12,14},{14,12},{16,18},{18,... | collective-permute-start | bytes 442376 | tf_op jit(solution)/shard_map/ppermute | solution.py:369
  31.3 0.4 collective-permute-start.9
  31.7 1.5 %collective-permute-start.10 = (bf16[576,128]{1,0:T(8,128)(2,1)S(1)}, bf16[576,128]{1,0:T(8,128)(2,1)S(1)}, u32[]{:S(2)}, u32[]{:S(2)}) collective-permute-start(bf16[576,128]{1,0:T(8,128)(2,1)S(1)} %get-tuple-element.46), channel_id=1, source_target_pairs={{0,6},{2,4},{4,2},{6,0},{8,14},{10,12},{12,10},{14,8},{16,22},{18,... | collective-permute-start | bytes 442376 | tf_op jit(solution)/shard_map/ppermute | solution.py:369
  33.3 3.1 %collective-permute-done.8.refs_1_ = bf16[576,128]{1,0:T(8,128)(2,1)S(1)} collective-permute-done((bf16[576,128]{1,0:T(8,128)(2,1)S(1)}, bf16[576,128]{1,0:T(8,128)(2,1)S(1)}, u32[]{:S(2)}, u32[]{:S(2)}) %collective-permute-start.8) | collective-permute-done | bytes 147488 | tf_op jit(solution)/shard_map/ppermute | solution.py:369
  36.4 2.0 %collective-permute-done.9.refs_2_ = bf16[576,128]{1,0:T(8,128)(2,1)S(1)} collective-permute-done((bf16[576,128]{1,0:T(8,128)(2,1)S(1)}, bf16[576,128]{1,0:T(8,128)(2,1)S(1)}, u32[]{:S(2)}, u32[]{:S(2)}) %collective-permute-start.9) | collective-permute-done | bytes 147488 | tf_op jit(solution)/shard_map/ppermute | solution.py:369
  38.3 1.8 %collective-permute-done.10.refs_3_ = bf16[576,128]{1,0:T(8,128)(2,1)S(1)} collective-permute-done((bf16[576,128]{1,0:T(8,128)(2,1)S(1)}, bf16[576,128]{1,0:T(8,128)(2,1)S(1)}, u32[]{:S(2)}, u32[]{:S(2)}) %collective-permute-start.10) | collective-permute-done | bytes 147488 | tf_op jit(solution)/shard_map/ppermute | solution.py:369
  40.1 0.1 sum.3.refs_0_
  40.2 1.6 %collective-permute-start.11 = (bf16[576,128]{1,0:T(8,128)(2,1)S(1)}, bf16[576,128]{1,0:T(8,128)(2,1)S(1)}, u32[]{:S(2)}, u32[]{:S(2)}) collective-permute-start(bf16[576,128]{1,0:T(8,128)(2,1)S(1)} %sum.3.refs_0_), channel_id=1, source_target_pairs={{0,8},{2,10},{4,12},{6,14},{8,0},{10,2},{12,4},{14,6},{16,24},{18,... | collective-permute-start | bytes 442376 | tf_op jit(solution)/shard_map/ppermute | solution.py:369
  41.8 3.6 %collective-permute-done.11.refs_1_ = bf16[576,128]{1,0:T(8,128)(2,1)S(1)} collective-permute-done((bf16[576,128]{1,0:T(8,128)(2,1)S(1)}, bf16[576,128]{1,0:T(8,128)(2,1)S(1)}, u32[]{:S(2)}, u32[]{:S(2)}) %collective-permute-start.11) | collective-permute-done | bytes 147488 | tf_op jit(solution)/shard_map/ppermute | solution.py:369
  45.5 2.6 %collective-permute-start.14 = (bf16[576,128]{1,0:T(8,128)(2,1)S(1)}, bf16[576,128]{1,0:T(8,128)(2,1)S(1)}, u32[]{:S(2)}, u32[]{:S(2)}) collective-permute-start(bf16[576,128]{1,0:T(8,128)(2,1)S(1)} %sum.4.refs_0_), channel_id=1, source_target_pairs={{0,16},{2,18},{4,20},{6,22},{8,24},{10,26},{12,28},{14,30},{16,0},... | collective-permute-start | bytes 442376 | tf_op jit(solution)/shard_map/ppermute | solution.py:369
  48.0 0.8 %inputs.1 = (f32[4,64,512]{2,1,0:T(8,128)S(1)}, bf16[2,64,512]{2,1,0:T(8,128)(2,1)S(1)}) custom-call(bf16[4096,256]{1,0:T(8,128)(2,1)S(1)} %get-tuple-element.48.td1, bf16[128,1536]{1,0:T(8,128)(2,1)S(1)} %get-tuple-element.49.wt1), custom_call_target="tpu_custom_call" | custom-call | flops 1000000 | bytes 100000 | tf_op jit(solution)/shard_map/inputs/pallas_call | solution.py:343
  48.8 0.6 collective-permute-start.13
  49.4 5.1 %collective-permute-start.12 = (bf16[64,512]{1,0:T(8,128)(2,1)S(1)}, bf16[64,512]{1,0:T(8,128)(2,1)S(1)}, u32[]{:S(2)}, u32[]{:S(2)}) collective-permute-start(bf16[64,512]{1,0:T(8,128)(2,1)S(1)} %get-tuple-element.67), channel_id=1, source_target_pairs={{2,0},{4,2},{6,4},{8,6},{10,8},{12,10},{14,12},{16,14},{18,16},{20... | collective-permute-start | bytes 196616 | tf_op jit(solution)/shard_map/ppermute | solution.py:442
  54.5 0.0 collective-permute-done.14.refs_1_
  54.6 1.1 %collective-permute-start.17 = (bf16[576,128]{1,0:T(8,128)(2,1)S(1)}, bf16[576,128]{1,0:T(8,128)(2,1)S(1)}, u32[]{:S(2)}, u32[]{:S(2)}) collective-permute-start(bf16[576,128]{1,0:T(8,128)(2,1)S(1)} %sum.5.p0), channel_id=1, source_target_pairs={{0,6},{2,4},{4,2},{6,0},{8,14},{10,12},{12,10},{14,8},{16,22},{18,... | collective-permute-start | bytes 442376 | tf_op jit(solution)/shard_map/ppermute | solution.py:369
  55.7 2.4 %collective-permute-start.15 = (bf16[576,128]{1,0:T(8,128)(2,1)S(1)}, bf16[576,128]{1,0:T(8,128)(2,1)S(1)}, u32[]{:S(2)}, u32[]{:S(2)}) collective-permute-start(bf16[576,128]{1,0:T(8,128)(2,1)S(1)} %sum.5.p0), channel_id=1, source_target_pairs={{0,2},{2,0},{4,6},{6,4},{8,10},{10,8},{12,14},{14,12},{16,18},{18,... | collective-permute-start | bytes 442376 | tf_op jit(solution)/shard_map/ppermute | solution.py:369
  58.1 0.0 collective-permute-done.13
  58.1 0.0 collective-permute-done.12
  58.2 0.4 fusion.1
  58.6 0.9 %copy.12 = bf16[64,4,512]{2,1,0:T(4,128)(2,1)} copy(bf16[64,4,512]{2,0,1:T(8,128)(2,1)S(1)} %fusion.1) | data formatting | bytes 524288
  59.5 1.3 %collective-permute-done.17.p3 = bf16[576,128]{1,0:T(8,128)(2,1)S(1)} collective-permute-done((bf16[576,128]{1,0:T(8,128)(2,1)S(1)}, bf16[576,128]{1,0:T(8,128)(2,1)S(1)}, u32[]{:S(2)}, u32[]{:S(2)}) %collective-permute-start.17) | collective-permute-done | bytes 147488 | tf_op jit(solution)/shard_map/ppermute | solution.py:369
  60.8 1.5 %collective-permute-done.16.p2 = bf16[576,128]{1,0:T(8,128)(2,1)S(1)} collective-permute-done((bf16[576,128]{1,0:T(8,128)(2,1)S(1)}, bf16[576,128]{1,0:T(8,128)(2,1)S(1)}, u32[]{:S(2)}, u32[]{:S(2)}) %collective-permute-start.16) | collective-permute-done | bytes 147488 | tf_op jit(solution)/shard_map/ppermute | solution.py:369
  62.3 1.6 %last.1 = (f32[1152,128]{1,0:T(8,128)}, f32[576,128]{1,0:T(8,128)}, f32[576,128]{1,0:T(8,128)}) custom-call(s32[2]{0:T(128)S(1)} %pad_add_fusion.core, bf16[576,128]{1,0:T(8,128)(2,1)S(1)} %sum.5.p0, bf16[576,128]{1,0:T(8,128)(2,1)S(1)} %collective-permute-done.15.p1, bf16[576,128]{1,0:T(8,128)(2,1)S(1)} %collective-permute-done.16.p2, ...), custom_call_target="tpu_custom_call" | custom-call | flops 1000000 | bytes 100000 | tf_op jit(solution)/shard_map/last/pallas_call | solution.py:343
  (21 shorter events, 0.3 us)
Async XLA Ops:
  0.6 2.4 %copy-start = (bf16[64,4,512]{2,1,0:T(4,128)(2,1)S(1)}, bf16[64,4,512]{2,1,0:T(4,128)(2,1)}, u32[]{:S(2)}) copy-start(bf16[64,4,512]{2,1,0:T(4,128)(2,1)} %param.6) | copy-start | bytes 786436
  0.6 10.2 %collective-permute-start.3 = (bf16[576,128]{1,0:T(8,128)(2,1)}, bf16[576,128]{1,0:T(8,128)(2,1)S(1)}, u32[]{:S(2)}, u32[]{:S(2)}) collective-permute-start(bf16[576,128]{1,0:T(8,128)(2,1)} %bitcast.34), channel_id=1, source_target_pairs={{0,1},{1,0},{2,3},{3,2},{4,5},{5,4},{6,7},{7,6},{8,9},{9,8},{10,11... | collective-permute-start | bytes 442376 | tf_op jit(solution)/shard_map/ppermute | solution.py:366
  1.2 11.0 %collective-permute-start.5 = (bf16[1152,128]{1,0:T(8,128)(2,1)}, bf16[1152,128]{1,0:T(8,128)(2,1)S(1)}, u32[]{:S(2)}, u32[]{:S(2)}) collective-permute-start(bf16[1152,128]{1,0:T(8,128)(2,1)} %bitcast.32), channel_id=1, source_target_pairs={{0,1},{1,0},{2,3},{3,2},{4,5},{5,4},{6,7},{7,6},{8,9},{9,8},{10,11... | collective-permute-start | bytes 884744 | tf_op jit(solution)/shard_map/ppermute | solution.py:366
  3.5 7.4 %copy-start.3 = (bf16[3,3,64,128]{3,2,1,0:T(8,128)(2,1)S(1)}, bf16[3,3,64,128]{3,2,1,0:T(8,128)(2,1)}, u32[]{:S(2)}) copy-start(bf16[3,3,64,128]{3,2,1,0:T(8,128)(2,1)} %param.8) | copy-start | bytes 442372
  3.5 8.7 %copy-start.1 = (bf16[3,3,128,128]{3,2,1,0:T(8,128)(2,1)S(1)}, bf16[3,3,128,128]{3,2,1,0:T(8,128)(2,1)}, u32[]{:S(2)}) copy-start(bf16[3,3,128,128]{3,2,1,0:T(8,128)(2,1)} %param.9) | copy-start | bytes 884740
  3.5 8.7 %copy-start.2 = (bf16[3,3,64,128]{3,2,1,0:T(8,128)(2,1)S(1)}, bf16[3,3,64,128]{3,2,1,0:T(8,128)(2,1)}, u32[]{:S(2)}) copy-start(bf16[3,3,64,128]{3,2,1,0:T(8,128)(2,1)} %param.7) | copy-start | bytes 442372
  3.5 8.7 %collective-permute-start.2 = (bf16[6,64,512]{2,1,0:T(8,128)(2,1)S(1)}, bf16[6,64,512]{2,1,0:T(8,128)(2,1)S(1)}, u32[]{:S(2)}, u32[]{:S(2)}) collective-permute-start(bf16[6,64,512]{2,1,0:T(8,128)(2,1)S(1)} %maximum_maximum_fusion.own), channel_id=1, source_target_pairs={{0,1},{1,0},{2,3},{3,2},{4,5},{5,4},{6,7},{7,6},{8,9},{9,8},{10,11... | collective-permute-start | bytes 1179656 | tf_op jit(solution)/shard_map/ppermute | solution.py:366
  4.1 14.4 %collective-permute-start = (bf16[4,64,512]{2,1,0:T(8,128)(2,1)S(1)}, bf16[4,64,512]{2,1,0:T(8,128)(2,1)S(1)}, u32[]{:S(2)}, u32[]{:S(2)}) collective-permute-start(bf16[4,64,512]{2,1,0:T(8,128)(2,1)S(1)} %pad_maximum_fusion.1), channel_id=1, source_target_pairs={{0,2},{2,4},{4,6},{6,8},{8,10},{10,12},{12,14},{14,16},{16,18},{18... | collective-permute-start | bytes 786440 | tf_op jit(solution)/shard_map/ppermute | solution.py:385
  6.7 13.7 %collective-permute-start.1 = (bf16[4,64,512]{2,1,0:T(8,128)(2,1)S(1)}, bf16[4,64,512]{2,1,0:T(8,128)(2,1)S(1)}, u32[]{:S(2)}, u32[]{:S(2)}) collective-permute-start(bf16[4,64,512]{2,1,0:T(8,128)(2,1)S(1)} %fusion.5), channel_id=1, source_target_pairs={{2,0},{4,2},{6,4},{8,6},{10,8},{12,10},{14,12},{16,14},{18,16},{20... | collective-permute-start | bytes 786440 | tf_op jit(solution)/shard_map/ppermute | solution.py:386
  10.8 1.4 %collective-permute-start.4 = (bf16[576,128]{1,0:T(8,128)(2,1)S(1)}, bf16[576,128]{1,0:T(8,128)(2,1)S(1)}, u32[]{:S(2)}, u32[]{:S(2)}) collective-permute-start(bf16[576,128]{1,0:T(8,128)(2,1)S(1)} %bitcast.36), channel_id=1, source_target_pairs={{0,1},{1,0},{2,3},{3,2},{4,5},{5,4},{6,7},{7,6},{8,9},{9,8},{10,11... | collective-permute-start | bytes 442376 | tf_op jit(solution)/shard_map/ppermute | solution.py:366
  20.5 1.5 %collective-permute-start.6 = (bf16[4,64,512]{2,1,0:T(8,128)(2,1)S(1)}, bf16[4,64,512]{2,1,0:T(8,128)(2,1)S(1)}, u32[]{:S(2)}, u32[]{:S(2)}) collective-permute-start(bf16[4,64,512]{2,1,0:T(8,128)(2,1)S(1)} %collective-permute-done.own_before), channel_id=1, source_target_pairs={{0,1},{1,0},{2,3},{3,2},{4,5},{5,4},{6,7},{7,6},{8,9},{9,8},{10,11... | collective-permute-start | bytes 786440 | tf_op jit(solution)/shard_map/ppermute | solution.py:366
  20.5 1.9 %collective-permute-start.7 = (bf16[4,64,512]{2,1,0:T(8,128)(2,1)S(1)}, bf16[4,64,512]{2,1,0:T(8,128)(2,1)S(1)}, u32[]{:S(2)}, u32[]{:S(2)}) collective-permute-start(bf16[4,64,512]{2,1,0:T(8,128)(2,1)S(1)} %collective-permute-done.1.own_after), channel_id=1, source_target_pairs={{0,1},{1,0},{2,3},{3,2},{4,5},{5,4},{6,7},{7,6},{8,9},{9,8},{10,11... | collective-permute-start | bytes 786440 | tf_op jit(solution)/shard_map/ppermute | solution.py:366
  29.7 6.7 %collective-permute-start.8 = (bf16[576,128]{1,0:T(8,128)(2,1)S(1)}, bf16[576,128]{1,0:T(8,128)(2,1)S(1)}, u32[]{:S(2)}, u32[]{:S(2)}) collective-permute-start(bf16[576,128]{1,0:T(8,128)(2,1)S(1)} %get-tuple-element.44), channel_id=1, source_target_pairs={{0,2},{2,0},{4,6},{6,4},{8,10},{10,8},{12,14},{14,12},{16,18},{18,... | collective-permute-start | bytes 442376 | tf_op jit(solution)/shard_map/ppermute | solution.py:369
  31.3 7.0 %collective-permute-start.9 = (bf16[576,128]{1,0:T(8,128)(2,1)S(1)}, bf16[576,128]{1,0:T(8,128)(2,1)S(1)}, u32[]{:S(2)}, u32[]{:S(2)}) collective-permute-start(bf16[576,128]{1,0:T(8,128)(2,1)S(1)} %get-tuple-element.45), channel_id=1, source_target_pairs={{0,4},{2,6},{4,0},{6,2},{8,12},{10,14},{12,8},{14,10},{16,20},{18,... | collective-permute-start | bytes 442376 | tf_op jit(solution)/shard_map/ppermute | solution.py:369
  31.7 8.4 %collective-permute-start.10 = (bf16[576,128]{1,0:T(8,128)(2,1)S(1)}, bf16[576,128]{1,0:T(8,128)(2,1)S(1)}, u32[]{:S(2)}, u32[]{:S(2)}) collective-permute-start(bf16[576,128]{1,0:T(8,128)(2,1)S(1)} %get-tuple-element.46), channel_id=1, source_target_pairs={{0,6},{2,4},{4,2},{6,0},{8,14},{10,12},{12,10},{14,8},{16,22},{18,... | collective-permute-start | bytes 442376 | tf_op jit(solution)/shard_map/ppermute | solution.py:369
  40.2 5.2 %collective-permute-start.11 = (bf16[576,128]{1,0:T(8,128)(2,1)S(1)}, bf16[576,128]{1,0:T(8,128)(2,1)S(1)}, u32[]{:S(2)}, u32[]{:S(2)}) collective-permute-start(bf16[576,128]{1,0:T(8,128)(2,1)S(1)} %sum.3.refs_0_), channel_id=1, source_target_pairs={{0,8},{2,10},{4,12},{6,14},{8,0},{10,2},{12,4},{14,6},{16,24},{18,... | collective-permute-start | bytes 442376 | tf_op jit(solution)/shard_map/ppermute | solution.py:369
  45.5 9.1 %collective-permute-start.14 = (bf16[576,128]{1,0:T(8,128)(2,1)S(1)}, bf16[576,128]{1,0:T(8,128)(2,1)S(1)}, u32[]{:S(2)}, u32[]{:S(2)}) collective-permute-start(bf16[576,128]{1,0:T(8,128)(2,1)S(1)} %sum.4.refs_0_), channel_id=1, source_target_pairs={{0,16},{2,18},{4,20},{6,22},{8,24},{10,26},{12,28},{14,30},{16,0},... | collective-permute-start | bytes 442376 | tf_op jit(solution)/shard_map/ppermute | solution.py:369
  48.8 9.3 %collective-permute-start.13 = (bf16[64,512]{1,0:T(8,128)(2,1)S(1)}, bf16[64,512]{1,0:T(8,128)(2,1)S(1)}, u32[]{:S(2)}, u32[]{:S(2)}) collective-permute-start(bf16[64,512]{1,0:T(8,128)(2,1)S(1)} %get-tuple-element.66), channel_id=1, source_target_pairs={{0,2},{2,4},{4,6},{6,8},{8,10},{10,12},{12,14},{14,16},{16,18},{18... | collective-permute-start | bytes 196616 | tf_op jit(solution)/shard_map/ppermute | solution.py:443
  49.4 8.7 %collective-permute-start.12 = (bf16[64,512]{1,0:T(8,128)(2,1)S(1)}, bf16[64,512]{1,0:T(8,128)(2,1)S(1)}, u32[]{:S(2)}, u32[]{:S(2)}) collective-permute-start(bf16[64,512]{1,0:T(8,128)(2,1)S(1)} %get-tuple-element.67), channel_id=1, source_target_pairs={{2,0},{4,2},{6,4},{8,6},{10,8},{12,10},{14,12},{16,14},{18,16},{20... | collective-permute-start | bytes 196616 | tf_op jit(solution)/shard_map/ppermute | solution.py:442
  54.6 6.2 %collective-permute-start.17 = (bf16[576,128]{1,0:T(8,128)(2,1)S(1)}, bf16[576,128]{1,0:T(8,128)(2,1)S(1)}, u32[]{:S(2)}, u32[]{:S(2)}) collective-permute-start(bf16[576,128]{1,0:T(8,128)(2,1)S(1)} %sum.5.p0), channel_id=1, source_target_pairs={{0,6},{2,4},{4,2},{6,0},{8,14},{10,12},{12,10},{14,8},{16,22},{18,... | collective-permute-start | bytes 442376 | tf_op jit(solution)/shard_map/ppermute | solution.py:369
  55.7 6.6 %collective-permute-start.16 = (bf16[576,128]{1,0:T(8,128)(2,1)S(1)}, bf16[576,128]{1,0:T(8,128)(2,1)S(1)}, u32[]{:S(2)}, u32[]{:S(2)}) collective-permute-start(bf16[576,128]{1,0:T(8,128)(2,1)S(1)} %sum.5.p0), channel_id=1, source_target_pairs={{0,4},{2,6},{4,0},{6,2},{8,12},{10,14},{12,8},{14,10},{16,20},{18,... | collective-permute-start | bytes 442376 | tf_op jit(solution)/shard_map/ppermute | solution.py:369
  55.7 6.6 %collective-permute-start.15 = (bf16[576,128]{1,0:T(8,128)(2,1)S(1)}, bf16[576,128]{1,0:T(8,128)(2,1)S(1)}, u32[]{:S(2)}, u32[]{:S(2)}) collective-permute-start(bf16[576,128]{1,0:T(8,128)(2,1)S(1)} %sum.5.p0), channel_id=1, source_target_pairs={{0,2},{2,0},{4,6},{6,4},{8,10},{10,8},{12,14},{14,12},{16,18},{18,... | collective-permute-start | bytes 442376 | tf_op jit(solution)/shard_map/ppermute | solution.py:369

commit v2 on v1

--- a/solution.py
+++ b/solution.py
@@ -106,25 +106,34 @@
             base += size
 
 
-def put_input(ref, base, me, own, other):
-    m = own.shape[1] // 2
-    h = own.shape[0]
-    for at, row in ((me, own), (1 - me, other)):
-        even, odd = row[:, :m], row[:, m:]
-        blocks = (moved_right(odd.astype(F32)).astype(BF), even, odd, moved_left(even.astype(F32)).astype(BF))
-        for k, block in enumerate(blocks):
-            ref[pl.ds(pl.multiple_of(base + k * 2 * h + at * h, h), h), :] = block
-
-
-def put_cotangent(ref, base, me, own, other):
-    m = own.shape[1] // 2
-    h = own.shape[0]
-    for at, row in ((me, own), (1 - me, other)):
-        for k in range(2):
-            block = row[:, k * m : (k + 1) * m]
-            to = base + at * 2 * h + k * h
-            ref[pl.ds(pl.multiple_of(to, h), h), :] = block
-            ref[pl.ds(pl.multiple_of(to + 4 * h, h), h), :] = moved_left(block.astype(F32)).astype(BF)
+def put_input(ref, base, at, row):
+    h, m = row.shape[0], row.shape[1] // 2
+    even, odd = row[:, :m], row[:, m:]
+    blocks = (moved_right(odd.astype(F32)).astype(BF), even, odd, moved_left(even.astype(F32)).astype(BF))
+    for k, block in enumerate(blocks):
+        ref[pl.ds(pl.multiple_of(base + k * 2 * h + at * h, h), h), :] = block
+
+
+def put_cotangent(ref, base, at, row):
+    h, m = row.shape[0], row.shape[1] // 2
+    for k in range(2):
+        block = row[:, k * m : (k + 1) * m]
+        to = base + at * 2 * h + k * h
+        ref[pl.ds(pl.multiple_of(to, h), h), :] = block
+        ref[pl.ds(pl.multiple_of(to + 4 * h, h), h), :] = moved_left(block.astype(F32)).astype(BF)
+
+
+def put_outer(tx, tu, at, before, after):
+    stack = tx.shape[0] // 6
+    for k in range(3):
+        put_input(tx, k * stack, at, before[k])
+        put_input(tx, (k + 3) * stack, at, after[k])
+    put_cotangent(tu, 0, at, before[3])
+    put_cotangent(tu, stack, at, after[3])
+
+
+def outer_kernel(core, before, after, tx, tu):
+    put_outer(tx, tu, core[0], before, after)
 
 
 def inner_kernel(
@@ -137,9 +146,11 @@
     rows = own.shape[0] // 3 * 2
     put_weights(me, w1, other1, w2, other2, w3, other3, wb1, wb2, wt2, wt1, wt3e, wt3o)
     for r in range(rows):
-        put_input(tx, r * stack, me, own[r], other[r])
+        put_input(tx, r * stack, me, own[r])
+        put_input(tx, r * stack, 1 - me, other[r])
     for r in range(rows // 2):
-        put_cotangent(tu, r * stack, me, own[rows + r], other[rows + r])
+        put_cotangent(tu, r * stack, me, own[rows + r])
+        put_cotangent(tu, r * stack, 1 - me, other[rows + r])
 
     def first_dot(r):
         return dot(wb1[...], tx[pl.ds((r - 1) * stack, 3 * stack), :])
@@ -163,7 +174,7 @@
 
 
 def main_kernel(
-    core, own_before, before, own_after, after, wb1, wb2, wt2, wt3e, wt3o, txi, tui, th1i, dz1i, g2i,
+    core, _txo, _tuo, before, after, wb1, wb2, wt2, wt3e, wt3o, txi, tui, th1i, dz1i, g2i,
     p0, p1, p2, p3, td1, txo, tuo, th1o, dz1o, dz2, th2, td2, s2, s1, dw1, dw2, dw3,
 ):
     me = core[0]
@@ -283,14 +294,7 @@
     tasks += [z2[r] for r in range(1, rows)] + [g2[-1], z2[rows]] + [g2[r] for r in range(rows)]
     tasks += [w3[0], g1[0], g2[rows], w3[1]] + [g1[r] for r in range(1, rows - 1)] + [w3[2], g1[rows - 1], w2, w1]
 
-    for r in (-3, -2, -1):
-        ref, base = input_at(r)
-        put_input(ref, base, me, own_before[r + 3], before[r + 3])
-    for r in range(rows, rows + 3):
-        ref, base = input_at(r)
-        put_input(ref, base, me, own_after[r - rows], after[r - rows])
-    put_cotangent(tuo, 0, me, own_before[3], before[3])
-    put_cotangent(tuo, stack, me, own_after[3], after[3])
+    put_outer(txo, tuo, 1 - me, before, after)
     for out in (s2, s1):
         for par in range(2):
             out[par, pl.ds(0, 2 * h), :] = jnp.zeros((2 * h, m), BF)
@@ -327,7 +331,7 @@
     refs[-1][...] = total.astype(BF)
 
 
-def last_kernel(scales, core, p0, p1, p2, p3, *outs):
+def last_kernel(scales, core, p0, p3, p2, p1, *outs):
     for k, piece in enumerate((p0, p1, p2, p3)):
         at = piece_at(core[1], k)
         base = 0
@@ -337,7 +341,7 @@
             base += size
 
 
-def call(body, name, outs, scratch, limit, *args):
+def call(body, name, outs, scratch, limit, *args, aliases=None):
     vmem = pl.BlockSpec(memory_space=pltpu.VMEM)
     scalar = pl.BlockSpec(memory_space=pltpu.SMEM)
     return pl.pallas_call(
@@ -348,6 +352,7 @@
         scratch_shapes=[pltpu.VMEM(shape, kind) for shape, kind in scratch],
         compiler_params=pltpu.CompilerParams(vmem_limit_bytes=limit * 1024 * 1024),
         cost_estimate=pl.CostEstimate(flops=10**6, bytes_accessed=10**5, transcendentals=0),
+        input_output_aliases=aliases or {},
         name=name,
     )(*args)
 
@@ -407,14 +412,14 @@
         [], 24, core, own, across(own), *weights,
     )
     before, after, _ = lax.optimization_barrier((before, after, g2))
+    outer = [((6 * stack, m), BF), ((2 * stack, m), BF)]
+    txo, tuo = call(outer_kernel, "outer", outer, [], 8, core, before, after)
 
     size = 9 * (c + 2 * h) // 4
-    *parts, td1 = call(
+    *parts, td1, _, _ = call(
         main_kernel, "main",
-        [((size, c), BF)] * 4 + [(((rows + 4) * stack, m), BF)],
+        [((size, c), BF)] * 4 + [(((rows + 4) * stack, m), BF)] + outer,
         [
-            ((6 * stack, m), BF),
-            ((2 * stack, m), BF),
             ((6 * stack, m), BF),
             ((2 * 2 * c, m), F32),
             (((rows + 2) * 2 * c, m), F32),
@@ -426,7 +431,8 @@
             ((9 * h, c), BF),
             ((9 * c, c), BF),
         ],
-        32, core, before, across(before), after, across(after), wb1, wb2, wt2, wt3e, wt3o, tx, tu, th1, dz1, g2,
+        32, core, txo, tuo, across(before), across(after), wb1, wb2, wt2, wt3e, wt3o, tx, tu, th1, dz1, g2,
+        aliases={1: 5, 2: 6},
     )
     mine = total(parts[0], *[swapped(part, k) for k, part in enumerate(parts[1:], 1)])
     bit = 4
@@ -441,7 +447,8 @@
     )
     from_next = lax.ppermute(rims[0], "blk", down)
     from_prev = lax.ppermute(rims[1], "blk", up)
-    from_next, from_prev, _ = lax.optimization_barrier((from_next, from_prev, mine))
+    from_next, _ = lax.optimization_barrier((from_next, mine))
+    from_prev, _ = lax.optimization_barrier((from_prev, from_next))
     from_next, from_prev = from_next.astype(F32), from_prev.astype(F32)
     main = jnp.concatenate([main[:1] + from_prev, main[1:-1], main[-1:] + from_next]).astype(BF)
     grad_inputs = jnp.einsum("rin,cn->irc", main, split, preferred_element_type=F32).astype(BF)
@@ -451,7 +458,7 @@
     third, second, first = call(
         functools.partial(last_kernel, (wide, narrow, narrow)), "last",
         [((9 * c, c), F32), ((9 * h, c), F32), ((9 * h, c), F32)], [], 16,
-        core, mine, *[swapped(mine, k) for k in range(1, 4)],
+        core, mine, *[swapped(mine, k) for k in (3, 2, 1)],
     )
     return grad_inputs, first.reshape(3, 3, h, c), second.reshape(3, 3, h, c), third.reshape(3, 3, c, c)
 

time: 64.1 us -> 63.6 us (level)
  starting transfers between devices: 25.4 us -> 21.9 us
  waiting for transfers between devices: 21.8 us -> 24.1 us
    ppermute x1, starting transfers between devices: 5.09 us -> 2.23 us  [shards(): from_next = lax.ppermute(rims[0], 'blk', down)]
    ppermute x8, waiting for transfers between devices: 13.3 us -> 15.1 us  [swapped(): return lax.ppermute(piece, 'blk', [(i, i ^ k) for i in range(tiles)])]
    ppermute x1, waiting for transfers between devices: 0.01 us -> 1.21 us  [shards(): from_prev = lax.ppermute(rims[1], 'blk', up)]
    ppermute x6, waiting for transfers between devices: 2.54 us -> 1.78 us  [across(): return lax.ppermute(piece, 'chan', [(0, 1), (1, 0)])]
    pallas_call x7 -> x8, Pallas kernels: 12.2 us -> 12.8 us  [call(): pl.pallas_call(body, out_shape=tuple((jax.ShapeDtypeStruct(shape, kind) f...]
  transfers between devices with their start and end apart: 18 -> 18, of which waited for: 11 -> 12; matrix products, arithmetic and copies ran while one was open for 5% -> 5% of each run, Pallas kernels for 5% -> 6%
where the time goes in v2:
time: 63.6 us; the launch traced here: 63.4 us
  waiting for transfers between devices  24.1 us (38%)
  starting transfers between devices  21.9 us (34%)
  Pallas kernels  12.8 us (20%)
  matrix products  1.89 us (3%)
  between operations  1.48 us (2%)
  local copies, waits for them, and re-layouts  1 us (2%)
    ppermute x8, waiting for transfers between devices, swapped(): return lax.ppermute(piece, 'blk', [(i, i ^ k) for i in range(tiles)])  15.1 us
    pallas_call x8, Pallas kernels, call(): pl.pallas_call(body, out_shape=tuple((jax.ShapeDtypeStruct(shape, kind) f...  12.8 us
    ppermute x8, starting transfers between devices, swapped(): return lax.ppermute(piece, 'blk', [(i, i ^ k) for i in range(tiles)])  11.2 us
    ppermute x1, starting transfers between devices, shards(): after = lax.ppermute(jnp.concatenate([x[:3], u[:1]]), 'blk', down)  4.07 us
    ppermute x1, waiting for transfers between devices, shards(): lax.ppermute(jnp.concatenate([x[rows - 3:], u[rows // 2 - 1:]]), 'blk', up)  4.03 us
    ppermute x1, starting transfers between devices, shards(): lax.ppermute(jnp.concatenate([x[rows - 3:], u[rows // 2 - 1:]]), 'blk', up)  2.62 us
    ppermute x1, starting transfers between devices, shards(): from_next = lax.ppermute(rims[0], 'blk', down)  2.23 us
    ppermute x1, waiting for transfers between devices, shards(): after = lax.ppermute(jnp.concatenate([x[:3], u[:1]]), 'blk', down)  1.95 us
  transfers between devices with their start and end apart: 18, of which 12 were waited for; matrix products, arithmetic and copies ran while one was open for 5% of the time, Pallas kernels for 6%

profile of v2, /device:TPU:0, one launch (start us, length us, event | category | flops | bytes accessed | tf_op | source)
XLA Modules:
  0.0 63.4 jit_solution(13292557343830469785)
XLA Ops:
  0.6 0.0 copy-start
  0.6 0.5 collective-permute-start.3
  1.2 0.1 collective-permute-start.5
  1.9 1.1 %fusion.2 = bf16[2,128,256]{2,1,0:T(8,128)(2,1)S(1)} fusion(bf16[128,2,256]{2,1,0:T(2,128)(2,1)} %param.10, s32[256]{0:T(256)S(1)} %iota_select_fusion), kind=kOutput, calls=%fused_computation.6 | convolution fusion | flops 33685504 | bytes 263168 | tf_op jit(solution)/shard_map/orc,cn->ron/dot_general | solution.py:388
  3.1 0.4 fusion
  3.5 0.0 copy-start.3
  3.5 0.0 copy-start.1
  3.5 0.0 copy-start.2
  3.5 0.5 collective-permute-start.2
  4.1 2.6 %collective-permute-start = (bf16[4,64,512]{2,1,0:T(8,128)(2,1)S(1)}, bf16[4,64,512]{2,1,0:T(8,128)(2,1)S(1)}, u32[]{:S(2)}, u32[]{:S(2)}) collective-permute-start(bf16[4,64,512]{2,1,0:T(8,128)(2,1)S(1)} %pad_maximum_fusion.1), channel_id=1, source_target_pairs={{0,2},{2,4},{4,6},{6,8},{8,10},{10,12},{12,14},{14,16},{16,18},{18... | collective-permute-start | bytes 786440 | tf_op jit(solution)/shard_map/ppermute | solution.py:390
  6.7 4.1 %collective-permute-start.1 = (bf16[4,64,512]{2,1,0:T(8,128)(2,1)S(1)}, bf16[4,64,512]{2,1,0:T(8,128)(2,1)S(1)}, u32[]{:S(2)}, u32[]{:S(2)}) collective-permute-start(bf16[4,64,512]{2,1,0:T(8,128)(2,1)S(1)} %fusion.5), channel_id=1, source_target_pairs={{2,0},{4,2},{6,4},{8,6},{10,8},{12,10},{14,12},{16,14},{18,16},{20... | collective-permute-start | bytes 786440 | tf_op jit(solution)/shard_map/ppermute | solution.py:391
  10.8 0.0 collective-permute-done.3.other1
  10.8 0.2 collective-permute-start.4
  11.0 0.1 pad_add_fusion.core
  11.1 1.1 %collective-permute-done.4.other2 = bf16[576,128]{1,0:T(8,128)(2,1)S(1)} collective-permute-done((bf16[576,128]{1,0:T(8,128)(2,1)S(1)}, bf16[576,128]{1,0:T(8,128)(2,1)S(1)}, u32[]{:S(2)}, u32[]{:S(2)}) %collective-permute-start.4) | collective-permute-done | bytes 147488 | tf_op jit(solution)/shard_map/ppermute | solution.py:371
  12.2 0.0 collective-permute-done.5.other3
  12.2 2.3 %inner.1 = (bf16[256,1536]{1,0:T(8,128)(2,1)S(1)}, bf16[256,1536]{1,0:T(8,128)(2,1)S(1)}, bf16[256,1536]{1,0:T(8,128)(2,1)S(1)}, bf16[128,1536]{1,0:T(8,128)(2,1...) custom-call(s32[2]{0:T(128)S(1)} %pad_add_fusion.core, ...), custom_call_target="tpu_custom_call" | custom-call | flops 1000000 | bytes 100000 | tf_op jit(solution)/shard_map/inner/pallas_call | solution.py:347
  14.5 4.0 %collective-permute-done.before = bf16[4,64,512]{2,1,0:T(8,128)(2,1)S(1)} collective-permute-done((bf16[4,64,512]{2,1,0:T(8,128)(2,1)S(1)}, bf16[4,64,512]{2,1,0:T(8,128)(2,1)S(1)}, u32[]{:S(2)}, u32[]{:S(2)}) %collective-permute-start) | collective-permute-done | bytes 262176 | tf_op jit(solution)/shard_map/ppermute | solution.py:390
  18.5 1.9 %collective-permute-done.1.after = bf16[4,64,512]{2,1,0:T(8,128)(2,1)S(1)} collective-permute-done((bf16[4,64,512]{2,1,0:T(8,128)(2,1)S(1)}, bf16[4,64,512]{2,1,0:T(8,128)(2,1)S(1)}, u32[]{:S(2)}, u32[]{:S(2)}) %collective-permute-start.1) | collective-permute-done | bytes 262176 | tf_op jit(solution)/shard_map/ppermute | solution.py:391
  20.5 0.0 collective-permute-start.6
  20.5 0.5 collective-permute-start.7
  21.0 0.8 %outer.1 = (bf16[3072,256]{1,0:T(8,128)(2,1)S(1)}, bf16[1024,256]{1,0:T(8,128)(2,1)S(1)}) custom-call(s32[2]{0:T(128)S(1)} %pad_add_fusion.core, bf16[4,64,512]{2,1,0:T(8,128)(2,1)S(1)} %collective-permute-done.before, bf16[4,64,512]{2,1,0:T(8,128)(2,1)S(1)} %collective-permute-done.1.after), custom_call_target="tpu_custom_call" | custom-call | flops 1000000 | bytes 100000 | tf_op jit(solution)/shard_map/outer/pallas_call | solution.py:347
  21.7 0.3 collective-permute-done.6.before
  22.0 0.4 collective-permute-done.7.after
  22.4 7.3 %main.1 = (bf16[576,128]{1,0:T(8,128)(2,1)S(1)}, bf16[576,128]{1,0:T(8,128)(2,1)S(1)}, bf16[576,128]{1,0:T(8,128)(2,1)S(1)}, bf16[576,128]{1,0:T(8,128)(2,1)S(1)...) custom-call(s32[2]{0:T(128)S(1)} %pad_add_fusion.core, ...), custom_call_target="tpu_custom_call", output_to_operand_aliasing={{5}: (1, {}), {6}: (2, {})} | custom-call | flops 1000000 | bytes 100000 | tf_op jit(solution)/shard_map/main/pallas_call | solution.py:347
  29.6 1.6 %collective-permute-start.8 = (bf16[576,128]{1,0:T(8,128)(2,1)S(1)}, bf16[576,128]{1,0:T(8,128)(2,1)S(1)}, u32[]{:S(2)}, u32[]{:S(2)}) collective-permute-start(bf16[576,128]{1,0:T(8,128)(2,1)S(1)} %get-tuple-element.48), channel_id=1, source_target_pairs={{0,2},{2,0},{4,6},{6,4},{8,10},{10,8},{12,14},{14,12},{16,18},{18,... | collective-permute-start | bytes 442376 | tf_op jit(solution)/shard_map/ppermute | solution.py:374
  31.2 0.4 collective-permute-start.9
  31.6 1.6 %collective-permute-start.10 = (bf16[576,128]{1,0:T(8,128)(2,1)S(1)}, bf16[576,128]{1,0:T(8,128)(2,1)S(1)}, u32[]{:S(2)}, u32[]{:S(2)}) collective-permute-start(bf16[576,128]{1,0:T(8,128)(2,1)S(1)} %get-tuple-element.50), channel_id=1, source_target_pairs={{0,6},{2,4},{4,2},{6,0},{8,14},{10,12},{12,10},{14,8},{16,22},{18,... | collective-permute-start | bytes 442376 | tf_op jit(solution)/shard_map/ppermute | solution.py:374
  33.2 3.1 %collective-permute-done.8.refs_1_ = bf16[576,128]{1,0:T(8,128)(2,1)S(1)} collective-permute-done((bf16[576,128]{1,0:T(8,128)(2,1)S(1)}, bf16[576,128]{1,0:T(8,128)(2,1)S(1)}, u32[]{:S(2)}, u32[]{:S(2)}) %collective-permute-start.8) | collective-permute-done | bytes 147488 | tf_op jit(solution)/shard_map/ppermute | solution.py:374
  36.3 2.0 %collective-permute-done.9.refs_2_ = bf16[576,128]{1,0:T(8,128)(2,1)S(1)} collective-permute-done((bf16[576,128]{1,0:T(8,128)(2,1)S(1)}, bf16[576,128]{1,0:T(8,128)(2,1)S(1)}, u32[]{:S(2)}, u32[]{:S(2)}) %collective-permute-start.9) | collective-permute-done | bytes 147488 | tf_op jit(solution)/shard_map/ppermute | solution.py:374
  38.2 1.8 %collective-permute-done.10.refs_3_ = bf16[576,128]{1,0:T(8,128)(2,1)S(1)} collective-permute-done((bf16[576,128]{1,0:T(8,128)(2,1)S(1)}, bf16[576,128]{1,0:T(8,128)(2,1)S(1)}, u32[]{:S(2)}, u32[]{:S(2)}) %collective-permute-start.10) | collective-permute-done | bytes 147488 | tf_op jit(solution)/shard_map/ppermute | solution.py:374
  40.0 0.1 sum.3.refs_0_
  40.1 1.6 %collective-permute-start.11 = (bf16[576,128]{1,0:T(8,128)(2,1)S(1)}, bf16[576,128]{1,0:T(8,128)(2,1)S(1)}, u32[]{:S(2)}, u32[]{:S(2)}) collective-permute-start(bf16[576,128]{1,0:T(8,128)(2,1)S(1)} %sum.3.refs_0_), channel_id=1, source_target_pairs={{0,8},{2,10},{4,12},{6,14},{8,0},{10,2},{12,4},{14,6},{16,24},{18,... | collective-permute-start | bytes 442376 | tf_op jit(solution)/shard_map/ppermute | solution.py:374
  41.7 3.6 %collective-permute-done.11.refs_1_ = bf16[576,128]{1,0:T(8,128)(2,1)S(1)} collective-permute-done((bf16[576,128]{1,0:T(8,128)(2,1)S(1)}, bf16[576,128]{1,0:T(8,128)(2,1)S(1)}, u32[]{:S(2)}, u32[]{:S(2)}) %collective-permute-start.11) | collective-permute-done | bytes 147488 | tf_op jit(solution)/shard_map/ppermute | solution.py:374
  45.4 2.6 %collective-permute-start.14 = (bf16[576,128]{1,0:T(8,128)(2,1)S(1)}, bf16[576,128]{1,0:T(8,128)(2,1)S(1)}, u32[]{:S(2)}, u32[]{:S(2)}) collective-permute-start(bf16[576,128]{1,0:T(8,128)(2,1)S(1)} %sum.4.refs_0_), channel_id=1, source_target_pairs={{0,16},{2,18},{4,20},{6,22},{8,24},{10,26},{12,28},{14,30},{16,0},... | collective-permute-start | bytes 442376 | tf_op jit(solution)/shard_map/ppermute | solution.py:374
  48.0 0.8 %inputs.1 = (f32[4,64,512]{2,1,0:T(8,128)S(1)}, bf16[2,64,512]{2,1,0:T(8,128)(2,1)S(1)}) custom-call(bf16[4096,256]{1,0:T(8,128)(2,1)S(1)} %get-tuple-element.52.td1, bf16[128,1536]{1,0:T(8,128)(2,1)S(1)} %get-tuple-element.53.wt1), custom_call_target="tpu_custom_call" | custom-call | flops 1000000 | bytes 100000 | tf_op jit(solution)/shard_map/inputs/pallas_call | solution.py:347
  48.8 2.2 %collective-permute-start.13 = (bf16[64,512]{1,0:T(8,128)(2,1)S(1)}, bf16[64,512]{1,0:T(8,128)(2,1)S(1)}, u32[]{:S(2)}, u32[]{:S(2)}) collective-permute-start(bf16[64,512]{1,0:T(8,128)(2,1)S(1)} %get-tuple-element.71), channel_id=1, source_target_pairs={{2,0},{4,2},{6,4},{8,6},{10,8},{12,10},{14,12},{16,14},{18,16},{20... | collective-permute-start | bytes 196616 | tf_op jit(solution)/shard_map/ppermute | solution.py:448
  51.0 3.2 %collective-permute-done.14.refs_1_ = bf16[576,128]{1,0:T(8,128)(2,1)S(1)} collective-permute-done((bf16[576,128]{1,0:T(8,128)(2,1)S(1)}, bf16[576,128]{1,0:T(8,128)(2,1)S(1)}, u32[]{:S(2)}, u32[]{:S(2)}) %collective-permute-start.14) | collective-permute-done | bytes 147488 | tf_op jit(solution)/shard_map/ppermute | solution.py:374
  54.2 0.1 collective-permute-start.17
  54.3 1.2 %collective-permute-start.16 = (bf16[576,128]{1,0:T(8,128)(2,1)S(1)}, bf16[576,128]{1,0:T(8,128)(2,1)S(1)}, u32[]{:S(2)}, u32[]{:S(2)}) collective-permute-start(bf16[576,128]{1,0:T(8,128)(2,1)S(1)} %sum.5.p0), channel_id=1, source_target_pairs={{0,4},{2,6},{4,0},{6,2},{8,12},{10,14},{12,8},{14,10},{16,20},{18,... | collective-permute-start | bytes 442376 | tf_op jit(solution)/shard_map/ppermute | solution.py:374
  55.5 2.3 %collective-permute-start.15 = (bf16[576,128]{1,0:T(8,128)(2,1)S(1)}, bf16[576,128]{1,0:T(8,128)(2,1)S(1)}, u32[]{:S(2)}, u32[]{:S(2)}) collective-permute-start(bf16[576,128]{1,0:T(8,128)(2,1)S(1)} %sum.5.p0), channel_id=1, source_target_pairs={{0,6},{2,4},{4,2},{6,0},{8,14},{10,12},{12,10},{14,8},{16,22},{18,... | collective-permute-start | bytes 442376 | tf_op jit(solution)/shard_map/ppermute | solution.py:374
  57.8 0.0 collective-permute-done.13
  57.8 1.2 %collective-permute-done.12 = bf16[64,512]{1,0:T(8,128)(2,1)S(1)} collective-permute-done((bf16[64,512]{1,0:T(8,128)(2,1)S(1)}, bf16[64,512]{1,0:T(8,128)(2,1)S(1)}, u32[]{:S(2)}, u32[]{:S(2)}) %collective-permute-start.12) | collective-permute-done | bytes 65568 | tf_op jit(solution)/shard_map/ppermute | solution.py:449
  59.0 0.4 fusion.1
  59.5 0.9 %copy.14 = bf16[64,4,512]{2,1,0:T(4,128)(2,1)} copy(bf16[64,4,512]{2,0,1:T(8,128)(2,1)S(1)} %fusion.1) | data formatting | bytes 524288
  60.4 0.0 collective-permute-done.17.p1
  60.4 1.5 %collective-permute-done.16.p2 = bf16[576,128]{1,0:T(8,128)(2,1)S(1)} collective-permute-done((bf16[576,128]{1,0:T(8,128)(2,1)S(1)}, bf16[576,128]{1,0:T(8,128)(2,1)S(1)}, u32[]{:S(2)}, u32[]{:S(2)}) %collective-permute-start.16) | collective-permute-done | bytes 147488 | tf_op jit(solution)/shard_map/ppermute | solution.py:374
  61.8 1.6 %last.1 = (f32[1152,128]{1,0:T(8,128)}, f32[576,128]{1,0:T(8,128)}, f32[576,128]{1,0:T(8,128)}) custom-call(s32[2]{0:T(128)S(1)} %pad_add_fusion.core, bf16[576,128]{1,0:T(8,128)(2,1)S(1)} %sum.5.p0, bf16[576,128]{1,0:T(8,128)(2,1)S(1)} %collective-permute-done.15.p3, bf16[576,128]{1,0:T(8,128)(2,1)S(1)} %collective-permute-done.16.p2, ...), custom_call_target="tpu_custom_call" | custom-call | flops 1000000 | bytes 100000 | tf_op jit(solution)/shard_map/last/pallas_call | solution.py:347
  (22 shorter events, 0.3 us)
Async XLA Ops:
  0.6 2.4 %copy-start = (bf16[64,4,512]{2,1,0:T(4,128)(2,1)S(1)}, bf16[64,4,512]{2,1,0:T(4,128)(2,1)}, u32[]{:S(2)}) copy-start(bf16[64,4,512]{2,1,0:T(4,128)(2,1)} %param.6) | copy-start | bytes 786436
  0.6 10.2 %collective-permute-start.3 = (bf16[576,128]{1,0:T(8,128)(2,1)}, bf16[576,128]{1,0:T(8,128)(2,1)S(1)}, u32[]{:S(2)}, u32[]{:S(2)}) collective-permute-start(bf16[576,128]{1,0:T(8,128)(2,1)} %bitcast.34), channel_id=1, source_target_pairs={{0,1},{1,0},{2,3},{3,2},{4,5},{5,4},{6,7},{7,6},{8,9},{9,8},{10,11... | collective-permute-start | bytes 442376 | tf_op jit(solution)/shard_map/ppermute | solution.py:371
  1.2 11.0 %collective-permute-start.5 = (bf16[1152,128]{1,0:T(8,128)(2,1)}, bf16[1152,128]{1,0:T(8,128)(2,1)S(1)}, u32[]{:S(2)}, u32[]{:S(2)}) collective-permute-start(bf16[1152,128]{1,0:T(8,128)(2,1)} %bitcast.32), channel_id=1, source_target_pairs={{0,1},{1,0},{2,3},{3,2},{4,5},{5,4},{6,7},{7,6},{8,9},{9,8},{10,11... | collective-permute-start | bytes 884744 | tf_op jit(solution)/shard_map/ppermute | solution.py:371
  3.5 7.4 %copy-start.3 = (bf16[3,3,64,128]{3,2,1,0:T(8,128)(2,1)S(1)}, bf16[3,3,64,128]{3,2,1,0:T(8,128)(2,1)}, u32[]{:S(2)}) copy-start(bf16[3,3,64,128]{3,2,1,0:T(8,128)(2,1)} %param.8) | copy-start | bytes 442372
  3.5 8.7 %copy-start.1 = (bf16[3,3,128,128]{3,2,1,0:T(8,128)(2,1)S(1)}, bf16[3,3,128,128]{3,2,1,0:T(8,128)(2,1)}, u32[]{:S(2)}) copy-start(bf16[3,3,128,128]{3,2,1,0:T(8,128)(2,1)} %param.9) | copy-start | bytes 884740
  3.5 8.7 %copy-start.2 = (bf16[3,3,64,128]{3,2,1,0:T(8,128)(2,1)S(1)}, bf16[3,3,64,128]{3,2,1,0:T(8,128)(2,1)}, u32[]{:S(2)}) copy-start(bf16[3,3,64,128]{3,2,1,0:T(8,128)(2,1)} %param.7) | copy-start | bytes 442372
  3.5 8.7 %collective-permute-start.2 = (bf16[6,64,512]{2,1,0:T(8,128)(2,1)S(1)}, bf16[6,64,512]{2,1,0:T(8,128)(2,1)S(1)}, u32[]{:S(2)}, u32[]{:S(2)}) collective-permute-start(bf16[6,64,512]{2,1,0:T(8,128)(2,1)S(1)} %maximum_maximum_fusion.own), channel_id=1, source_target_pairs={{0,1},{1,0},{2,3},{3,2},{4,5},{5,4},{6,7},{7,6},{8,9},{9,8},{10,11... | collective-permute-start | bytes 1179656 | tf_op jit(solution)/shard_map/ppermute | solution.py:371
  4.1 14.4 %collective-permute-start = (bf16[4,64,512]{2,1,0:T(8,128)(2,1)S(1)}, bf16[4,64,512]{2,1,0:T(8,128)(2,1)S(1)}, u32[]{:S(2)}, u32[]{:S(2)}) collective-permute-start(bf16[4,64,512]{2,1,0:T(8,128)(2,1)S(1)} %pad_maximum_fusion.1), channel_id=1, source_target_pairs={{0,2},{2,4},{4,6},{6,8},{8,10},{10,12},{12,14},{14,16},{16,18},{18... | collective-permute-start | bytes 786440 | tf_op jit(solution)/shard_map/ppermute | solution.py:390
  6.7 13.7 %collective-permute-start.1 = (bf16[4,64,512]{2,1,0:T(8,128)(2,1)S(1)}, bf16[4,64,512]{2,1,0:T(8,128)(2,1)S(1)}, u32[]{:S(2)}, u32[]{:S(2)}) collective-permute-start(bf16[4,64,512]{2,1,0:T(8,128)(2,1)S(1)} %fusion.5), channel_id=1, source_target_pairs={{2,0},{4,2},{6,4},{8,6},{10,8},{12,10},{14,12},{16,14},{18,16},{20... | collective-permute-start | bytes 786440 | tf_op jit(solution)/shard_map/ppermute | solution.py:391
  10.8 1.4 %collective-permute-start.4 = (bf16[576,128]{1,0:T(8,128)(2,1)S(1)}, bf16[576,128]{1,0:T(8,128)(2,1)S(1)}, u32[]{:S(2)}, u32[]{:S(2)}) collective-permute-start(bf16[576,128]{1,0:T(8,128)(2,1)S(1)} %bitcast.36), channel_id=1, source_target_pairs={{0,1},{1,0},{2,3},{3,2},{4,5},{5,4},{6,7},{7,6},{8,9},{9,8},{10,11... | collective-permute-start | bytes 442376 | tf_op jit(solution)/shard_map/ppermute | solution.py:371
  20.5 1.5 %collective-permute-start.6 = (bf16[4,64,512]{2,1,0:T(8,128)(2,1)S(1)}, bf16[4,64,512]{2,1,0:T(8,128)(2,1)S(1)}, u32[]{:S(2)}, u32[]{:S(2)}) collective-permute-start(bf16[4,64,512]{2,1,0:T(8,128)(2,1)S(1)} %collective-permute-done.before), channel_id=1, source_target_pairs={{0,1},{1,0},{2,3},{3,2},{4,5},{5,4},{6,7},{7,6},{8,9},{9,8},{10,11... | collective-permute-start | bytes 786440 | tf_op jit(solution)/shard_map/ppermute | solution.py:371
  20.5 1.9 %collective-permute-start.7 = (bf16[4,64,512]{2,1,0:T(8,128)(2,1)S(1)}, bf16[4,64,512]{2,1,0:T(8,128)(2,1)S(1)}, u32[]{:S(2)}, u32[]{:S(2)}) collective-permute-start(bf16[4,64,512]{2,1,0:T(8,128)(2,1)S(1)} %collective-permute-done.1.after), channel_id=1, source_target_pairs={{0,1},{1,0},{2,3},{3,2},{4,5},{5,4},{6,7},{7,6},{8,9},{9,8},{10,11... | collective-permute-start | bytes 786440 | tf_op jit(solution)/shard_map/ppermute | solution.py:371
  29.6 6.6 %collective-permute-start.8 = (bf16[576,128]{1,0:T(8,128)(2,1)S(1)}, bf16[576,128]{1,0:T(8,128)(2,1)S(1)}, u32[]{:S(2)}, u32[]{:S(2)}) collective-permute-start(bf16[576,128]{1,0:T(8,128)(2,1)S(1)} %get-tuple-element.48), channel_id=1, source_target_pairs={{0,2},{2,0},{4,6},{6,4},{8,10},{10,8},{12,14},{14,12},{16,18},{18,... | collective-permute-start | bytes 442376 | tf_op jit(solution)/shard_map/ppermute | solution.py:374
  31.2 7.0 %collective-permute-start.9 = (bf16[576,128]{1,0:T(8,128)(2,1)S(1)}, bf16[576,128]{1,0:T(8,128)(2,1)S(1)}, u32[]{:S(2)}, u32[]{:S(2)}) collective-permute-start(bf16[576,128]{1,0:T(8,128)(2,1)S(1)} %get-tuple-element.49), channel_id=1, source_target_pairs={{0,4},{2,6},{4,0},{6,2},{8,12},{10,14},{12,8},{14,10},{16,20},{18,... | collective-permute-start | bytes 442376 | tf_op jit(solution)/shard_map/ppermute | solution.py:374
  31.6 8.4 %collective-permute-start.10 = (bf16[576,128]{1,0:T(8,128)(2,1)S(1)}, bf16[576,128]{1,0:T(8,128)(2,1)S(1)}, u32[]{:S(2)}, u32[]{:S(2)}) collective-permute-start(bf16[576,128]{1,0:T(8,128)(2,1)S(1)} %get-tuple-element.50), channel_id=1, source_target_pairs={{0,6},{2,4},{4,2},{6,0},{8,14},{10,12},{12,10},{14,8},{16,22},{18,... | collective-permute-start | bytes 442376 | tf_op jit(solution)/shard_map/ppermute | solution.py:374
  40.1 5.2 %collective-permute-start.11 = (bf16[576,128]{1,0:T(8,128)(2,1)S(1)}, bf16[576,128]{1,0:T(8,128)(2,1)S(1)}, u32[]{:S(2)}, u32[]{:S(2)}) collective-permute-start(bf16[576,128]{1,0:T(8,128)(2,1)S(1)} %sum.3.refs_0_), channel_id=1, source_target_pairs={{0,8},{2,10},{4,12},{6,14},{8,0},{10,2},{12,4},{14,6},{16,24},{18,... | collective-permute-start | bytes 442376 | tf_op jit(solution)/shard_map/ppermute | solution.py:374
  45.4 8.8 %collective-permute-start.14 = (bf16[576,128]{1,0:T(8,128)(2,1)S(1)}, bf16[576,128]{1,0:T(8,128)(2,1)S(1)}, u32[]{:S(2)}, u32[]{:S(2)}) collective-permute-start(bf16[576,128]{1,0:T(8,128)(2,1)S(1)} %sum.4.refs_0_), channel_id=1, source_target_pairs={{0,16},{2,18},{4,20},{6,22},{8,24},{10,26},{12,28},{14,30},{16,0},... | collective-permute-start | bytes 442376 | tf_op jit(solution)/shard_map/ppermute | solution.py:374
  48.8 9.0 %collective-permute-start.13 = (bf16[64,512]{1,0:T(8,128)(2,1)S(1)}, bf16[64,512]{1,0:T(8,128)(2,1)S(1)}, u32[]{:S(2)}, u32[]{:S(2)}) collective-permute-start(bf16[64,512]{1,0:T(8,128)(2,1)S(1)} %get-tuple-element.71), channel_id=1, source_target_pairs={{2,0},{4,2},{6,4},{8,6},{10,8},{12,10},{14,12},{16,14},{18,16},{20... | collective-permute-start | bytes 196616 | tf_op jit(solution)/shard_map/ppermute | solution.py:448
  51.0 8.0 %collective-permute-start.12 = (bf16[64,512]{1,0:T(8,128)(2,1)S(1)}, bf16[64,512]{1,0:T(8,128)(2,1)S(1)}, u32[]{:S(2)}, u32[]{:S(2)}) collective-permute-start(bf16[64,512]{1,0:T(8,128)(2,1)S(1)} %get-tuple-element.70), channel_id=1, source_target_pairs={{0,2},{2,4},{4,6},{6,8},{8,10},{10,12},{12,14},{14,16},{16,18},{18... | collective-permute-start | bytes 196616 | tf_op jit(solution)/shard_map/ppermute | solution.py:449
  54.2 6.1 %collective-permute-start.17 = (bf16[576,128]{1,0:T(8,128)(2,1)S(1)}, bf16[576,128]{1,0:T(8,128)(2,1)S(1)}, u32[]{:S(2)}, u32[]{:S(2)}) collective-permute-start(bf16[576,128]{1,0:T(8,128)(2,1)S(1)} %sum.5.p0), channel_id=1, source_target_pairs={{0,2},{2,0},{4,6},{6,4},{8,10},{10,8},{12,14},{14,12},{16,18},{18,... | collective-permute-start | bytes 442376 | tf_op jit(solution)/shard_map/ppermute | solution.py:374
  54.3 7.5 %collective-permute-start.16 = (bf16[576,128]{1,0:T(8,128)(2,1)S(1)}, bf16[576,128]{1,0:T(8,128)(2,1)S(1)}, u32[]{:S(2)}, u32[]{:S(2)}) collective-permute-start(bf16[576,128]{1,0:T(8,128)(2,1)S(1)} %sum.5.p0), channel_id=1, source_target_pairs={{0,4},{2,6},{4,0},{6,2},{8,12},{10,14},{12,8},{14,10},{16,20},{18,... | collective-permute-start | bytes 442376 | tf_op jit(solution)/shard_map/ppermute | solution.py:374
  55.5 6.3 %collective-permute-start.15 = (bf16[576,128]{1,0:T(8,128)(2,1)S(1)}, bf16[576,128]{1,0:T(8,128)(2,1)S(1)}, u32[]{:S(2)}, u32[]{:S(2)}) collective-permute-start(bf16[576,128]{1,0:T(8,128)(2,1)S(1)} %sum.5.p0), channel_id=1, source_target_pairs={{0,6},{2,4},{4,2},{6,0},{8,14},{10,12},{12,10},{14,8},{16,22},{18,... | collective-permute-start | bytes 442376 | tf_op jit(solution)/shard_map/ppermute | solution.py:374
